TPU v7x, 256 devices: a whole 4x4x8 slice. The times are simulated.
256 devices in a mesh: walk: 16 (over x, z_hi), chol: 16 (over y, z_lo, core).
Axes of the slice: x: 4, y: 4, z: 8 (z_hi: 4, z_lo: 2; z = z_hi * 2 + z_lo), core: 2. Of those that a mesh axis runs over, the one named last changes fastest.
Arguments:
- walkers: float32 [256, 640, 128], P(('walk', 'chol')), may hold values from -6 to 6
- intersection_inverse: float32 [256, 128, 128], P(('walk', 'chol')), may hold values from -0.2 to 1.2
- aux_draws: float32 [256, 3072], P(None, 'chol'), may hold values from -6 to 6
- chol_half: bfloat16 [3072, 640, 128], P('chol', 'walk'), may hold values from -0.01953125 to 0.01953125
- chol_full: bfloat16 [3072, 640, 640], P('chol', 'walk'), may hold values from -0.00390625 to 0.00390625
Outputs:
- new_walkers: float32 [256, 640, 128], P(('walk', 'chol'))
- aux_field: float32 [256, 3072], P(None, 'chol')
All inputs are finite; a program needn't handle non-finite values.
Results may differ from a plain program's by a relative error of at most 0.04.
Values may be sent and summed in bfloat16 or wider, within the bound.
A program may use at most 128 MiB of HBM per device.

v0:
```python
import jax
import jax.numpy as jnp
from jax import lax
from jax.sharding import PartitionSpec as P


def body(walkers, intersection_inverse, aux_draws, chol_half, chol_full):
    walk_size = lax.axis_size("walk")
    chol_size = lax.axis_size("chol")
    per_device, orbitals, electrons = walkers.shape
    slab_rows = orbitals // walk_size
    local_vectors = chol_half.shape[0]
    group_walkers = walk_size * per_device
    total_walkers = group_walkers * chol_size
    green_half = jnp.einsum(
        "wpj,wji->wpi", walkers, intersection_inverse, precision=lax.Precision.HIGHEST
    ).astype(jnp.bfloat16)
    green_slab = lax.all_to_all(green_half, "walk", split_axis=1, concat_axis=0, tiled=True)
    half_flat = chol_half.reshape(local_vectors, slab_rows * electrons)
    piece = lax.all_gather(green_slab, "chol", axis=0, tiled=True)
    flat_piece = piece.reshape(piece.shape[0], slab_rows * electrons)
    partial_bias = lax.dot_general(
        flat_piece, half_flat, (((1,), (1,)), ((), ())), preferred_element_type=jnp.float32
    )
    force_bias = lax.psum(partial_bias.astype(jnp.bfloat16), "walk").astype(jnp.float32)
    draws_sorted = aux_draws.reshape(walk_size, chol_size, per_device, local_vectors)
    draws_sorted = draws_sorted.transpose(1, 0, 2, 3).reshape(total_walkers, local_vectors)
    field_sorted = draws_sorted - force_bias
    aux_field = field_sorted.reshape(chol_size, walk_size, per_device, local_vectors)
    aux_field = aux_field.transpose(1, 0, 2, 3).reshape(total_walkers, local_vectors)
    field_low = field_sorted.astype(jnp.bfloat16)
    full_flat = chol_full.reshape(local_vectors, slab_rows * orbitals)
    summed = lax.psum_scatter(
        jnp.dot(field_low, full_flat, preferred_element_type=jnp.float32).astype(jnp.bfloat16),
        "chol",
        scatter_dimension=0,
        tiled=True,
    )
    operator = summed.reshape(group_walkers, slab_rows, orbitals)
    start_terms = lax.all_gather(walkers.astype(jnp.bfloat16), "walk", axis=0, tiled=True)
    taylor_term = jnp.einsum(
        "wrs,wsi->wri", operator, start_terms, preferred_element_type=jnp.float32
    )
    summed_terms = taylor_term
    for degree in range(2, 5):
        term_low = taylor_term.astype(jnp.bfloat16)
        taylor_term = (
            jnp.einsum(
                "wrs,wsi->wri",
                operator,
                lax.all_gather(term_low, "walk", axis=1, tiled=True),
                preferred_element_type=jnp.float32,
            )
            / degree
        )
        summed_terms = summed_terms + taylor_term
    returned = lax.all_to_all(
        summed_terms.astype(jnp.bfloat16), "walk", split_axis=0, concat_axis=1, tiled=True
    ).astype(summed_terms.dtype)
    new_walkers = walkers + returned
    return (new_walkers, aux_field)


def solution(mesh):
    placed = (
        P(("walk", "chol"), None, None),
        P(("walk", "chol"), None, None),
        P(None, "chol"),
        P("chol", "walk", None),
        P("chol", "walk", None),
    )
    return jax.shard_map(
        body,
        mesh=mesh,
        in_specs=placed,
        out_specs=(P(("walk", "chol"), None, None), P(None, "chol")),
        check_vma=False,
    )
```

profile of v0, /device:TPU:8, one launch (start us, length us, event | category | flops | bytes accessed | tf_op | source)
XLA Modules:
  0.0 675.3 jit_solution(7156987644610604160)
XLA Ops:
  7.2 1.5 fusion.7
  8.8 0.3 copy.46
  9.0 0.5 broadcast.3
  9.5 1.6 reduce
  11.2 22.1 %all_to_all.21 = bf16[16,2,2560]{2,1,0:T(2,128)(2,1)S(1)} all-to-all(bf16[16,2,2560]{2,1,0:T(2,128)(2,1)S(1)} %reshape.62), channel_id=1, replica_groups=mesh['walk'=16,'chol'=16] {'walk'}, dimensions={0} | all-to-all | bytes 327680 | tf_op jit(solution)/shard_map/all_to_all | solution.py:18
  33.4 0.7 copy.30
  34.2 36.7 %all-gather.6.cloned.1.call-done = bf16[256,40,128]{2,0,1:T(8,128)(2,1)} async-done(((bf16[16,40,128]{2,0,1:T(8,128)(2,1)}), bf16[256,40,128]{2,0,1:T(8,128)(2,1)}) %all-gather.6.cloned.1.call-update) | async-done | bytes 2621456 | tf_op jit(solution)/shard_map/all_gather | solution.py:20
  70.9 3.4 fusion.8
  74.4 0.1 copy.27
  74.5 0.2 copy.28
  74.8 9.3 %copy.37 = bf16[24,8,40,640]{3,1,2,0:T(8,128)(2,1)} copy(bf16[24,8,40,640]{3,2,1,0:T(8,128)(2,1)} %bitcast.48) | data formatting | bytes 19660800
  84.1 148.2 %all-reduce.2.cloned.1.call-done = bf16[256,192]{0,1:T(8,128)(2,1)} async-done(((bf16[256,192]{0,1:T(8,128)(2,1)}), bf16[256,192]{0,1:T(8,128)(2,1)}) %all-reduce.2.cloned.1.call-update) | async-done | bytes 98320 | tf_op jit(solution)/shard_map/psum | solution.py:25
  232.3 0.9 convert_subtract_fusion
  233.2 10.4 %convolution_convert_fusion = bf16[256,25600]{1,0:T(8,128)(2,1)} fusion(bf16[192,25600]{1,0:T(8,128)(2,1)} %bitcast.43, f32[256,192]{0,1:T(8,128)S(1)} %convert_subtract_fusion), kind=kOutput, calls=%fused_computation | convolution fusion | flops 2523185152 | bytes 23134208 | tf_op jit(solution)/shard_map/dot_general | solution.py:34
  243.8 0.9 copy-done.1
  244.7 0.7 convert_element_type.53
  245.4 141.3 %reduce-scatter.2.cloned.1.call-done = bf16[16,25600]{1,0:T(8,128)(2,1)} async-done(((bf16[256,25600]{1,0:T(8,128)(2,1)}), bf16[16,25600]{1,0:T(8,128)(2,1)}) %reduce-scatter.2.cloned.1.call-update) | async-done | bytes 819216 | tf_op jit(solution)/shard_map/reduce_scatter | solution.py:33
  386.7 1.2 copy.38
  387.9 65.9 %all-gather.8.cloned.1.call-done = bf16[16,640,128]{2,1,0:T(8,128)(2,1)} async-done(((bf16[1,640,128]{2,1,0:T(8,128)(2,1)}), bf16[16,640,128]{2,1,0:T(8,128)(2,1)}) %all-gather.8.cloned.1.call-update) | async-done | bytes 2621456 | tf_op jit(solution)/shard_map/all_gather | solution.py:40
  453.8 3.1 fusion.14
  457.0 60.2 %all-gather.10.cloned.1.call-done = bf16[16,640,128]{2,1,0:T(8,128)(2,1)} async-done(((bf16[16,40,128]{2,1,0:T(8,128)(2,1)}), bf16[16,640,128]{2,1,0:T(8,128)(2,1)}) %all-gather.10.cloned.1.call-update) | async-done | bytes 2621456 | tf_op jit(solution)/shard_map/all_gather | solution.py:51
  517.2 3.1 fusion.15
  520.4 61.3 %all-gather.12.cloned.1.call-done = bf16[16,640,128]{2,1,0:T(8,128)(2,1)} async-done(((bf16[16,40,128]{2,1,0:T(8,128)(2,1)}), bf16[16,640,128]{2,1,0:T(8,128)(2,1)}) %all-gather.12.cloned.1.call-update) | async-done | bytes 2621456 | tf_op jit(solution)/shard_map/all_gather | solution.py:51
  581.7 3.1 fusion.16
  584.9 61.5 %all-gather.14.cloned.1.call-done = bf16[16,640,128]{2,1,0:T(8,128)(2,1)} async-done(((bf16[16,40,128]{2,1,0:T(8,128)(2,1)}), bf16[16,640,128]{2,1,0:T(8,128)(2,1)}) %all-gather.14.cloned.1.call-update) | async-done | bytes 2621456 | tf_op jit(solution)/shard_map/all_gather | solution.py:51
  646.4 3.3 fusion.3
  649.6 7.1 %all-to-all-start.1 = ((bf16[16,40,128]{2,1,0:T(8,128)(2,1)}), bf16[16,40,128]{2,1,0:T(8,128)(2,1)S(1)}, u32[]{:S(2)}, u32[]{:S(2)}) async-start(bf16[16,40,128]{2,1,0:T(8,128)(2,1)} %fusion.3), calls=%async_computation.2 | async-start | bytes 327680 | tf_op jit(solution)/shard_map/all_to_all | solution.py:57
  656.7 0.1 copy.33
  656.9 0.2 copy.34
  657.0 0.8 copy.35
  657.8 9.9 %all-to-all-done.1 = bf16[16,40,128]{2,1,0:T(8,128)(2,1)S(1)} async-done(((bf16[16,40,128]{2,1,0:T(8,128)(2,1)}), bf16[16,40,128]{2,1,0:T(8,128)(2,1)S(1)}, u32[]{:S(2)}, u32[]{:S(2)}) %all-to-all-start.1) | async-done | bytes 163872 | tf_op jit(solution)/shard_map/all_to_all | solution.py:57
  667.7 0.8 convert_add_fusion
  (23 shorter events, 0.7 us)
Async XLA Ops:
  7.2 63.7 %copy-start = (bf16[192,40,128]{2,1,0:T(8,128)(2,1)S(1)}, bf16[192,40,128]{2,1,0:T(8,128)(2,1)}, u32[]{:S(2)}) copy-start(bf16[192,40,128]{2,1,0:T(8,128)(2,1)} %param.8) | copy-start | bytes 5898244
  7.2 63.7 %all-gather.6.cloned.1.call-start = ((), (), s32[]{:S(2)}) async-start(), calls=%async_computation.3 | async-start | bytes 2785280 | tf_op jit(solution)/shard_map/all_gather | solution.py:20
  34.1 40.2 %copy-start.2 = (f32[256,192]{0,1:T(8,128)S(1)}, f32[256,192]{0,1:T(8,128)}, u32[]{:S(2)}) copy-start(f32[256,192]{0,1:T(8,128)} %param.7) | copy-start | bytes 589828
  34.1 198.2 %all-reduce.2.cloned.1.call-start = ((), (), s32[]{:S(2)}) async-start(), calls=%async_computation.4 | async-start | bytes 196608 | tf_op jit(solution)/shard_map/psum | solution.py:25
  74.3 312.4 %reduce-scatter.2.cloned.1.call-start = ((), (), s32[]{:S(2)}) async-start(), calls=%async_computation.5 | async-start | bytes 13926400 | tf_op jit(solution)/shard_map/reduce_scatter | solution.py:33
  243.7 1.0 copy-start.1
  243.7 210.1 %all-gather.8.cloned.1.call-start = ((), (), s32[]{:S(2)}) async-start(), calls=%async_computation.6 | async-start | bytes 2785280 | tf_op jit(solution)/shard_map/all_gather | solution.py:40
  245.4 271.9 %all-gather.10.cloned.1.call-start = ((), (), s32[]{:S(2)}) async-start(), calls=%async_computation.7 | async-start | bytes 2785280 | tf_op jit(solution)/shard_map/all_gather | solution.py:51
  457.0 124.8 %all-gather.12.cloned.1.call-start = ((), (), s32[]{:S(2)}) async-start(), calls=%async_computation.8 | async-start | bytes 2785280 | tf_op jit(solution)/shard_map/all_gather | solution.py:51
  520.4 126.0 %all-gather.14.cloned.1.call-start = ((), (), s32[]{:S(2)}) async-start(), calls=%async_computation.9 | async-start | bytes 2785280 | tf_op jit(solution)/shard_map/all_gather | solution.py:51
  649.6 18.1 %all-to-all-start.1 = ((bf16[16,40,128]{2,1,0:T(8,128)(2,1)}), bf16[16,40,128]{2,1,0:T(8,128)(2,1)S(1)}, u32[]{:S(2)}, u32[]{:S(2)}) async-start(bf16[16,40,128]{2,1,0:T(8,128)(2,1)} %fusion.3), calls=%async_computation.2 | async-start | bytes 327680 | tf_op jit(solution)/shard_map/all_to_all | solution.py:57
Sparse Core Ops, SparseCore 0:
  34.3 36.5 all-gather.5
  74.4 157.8 all-reduce.1
  243.8 142.8 reduce-scatter.1
  389.9 63.8 all-gather.7
  457.1 60.0 all-gather.9
  520.5 61.2 all-gather.11
  585.1 61.2 all-gather.13
where the time goes:
time: 676 us; the launch traced here: 675 us
  waiting for transfers between devices  585 us (87%)
  matrix products  28 us (4%)
  blocking collectives  22.1 us (3%)
  local copies, waits for them, and re-layouts  14.6 us (2%)
  between operations  14.2 us (2%)
  starting transfers between devices  7.39 us (1%)
    all_gather x3, waiting for transfers between devices, body(): lax.all_gather(term_low, 'walk', axis=1, tiled=True)  183 us
    psum x1, waiting for transfers between devices, body(): lax.psum(partial_bias.astype(jnp.bfloat16), 'walk').astype(jnp.float32)  148 us
    reduce_scatter x1, waiting for transfers between devices, body(): lax.psum_scatter(jnp.dot(field_low, full_flat, preferred_element_type=jnp...  141 us
    all_gather x1, waiting for transfers between devices, body(): lax.all_gather(walkers.astype(jnp.bfloat16), 'walk', axis=0, tiled=True)  65.9 us
    all_gather x1, waiting for transfers between devices, body(): piece = lax.all_gather(green_slab, 'chol', axis=0, tiled=True)  36.7 us
    all_to_all x1, blocking collectives, body(): lax.all_to_all(green_half, 'walk', split_axis=1, concat_axis=0, tiled=True)  22.1 us
  transfers between devices with their start and end apart: 8, of which 8 were waited for; matrix products, arithmetic and copies ran while one was open for 2% of the time, Pallas kernels for 0%

commit v1 on v0

--- a/solution.py
+++ b/solution.py
@@ -22,7 +22,10 @@
     partial_bias = lax.dot_general(
         flat_piece, half_flat, (((1,), (1,)), ((), ())), preferred_element_type=jnp.float32
     )
-    force_bias = lax.psum(partial_bias.astype(jnp.bfloat16), "walk").astype(jnp.float32)
+    parts = partial_bias.astype(jnp.bfloat16).reshape(walk_size, -1, local_vectors)
+    parts = lax.all_to_all(parts, "walk", split_axis=0, concat_axis=0, tiled=True)
+    own_bias = jnp.sum(parts.astype(jnp.float32), axis=0).astype(jnp.bfloat16)
+    force_bias = lax.all_gather(own_bias, "walk", axis=0, tiled=True).astype(jnp.float32)
     draws_sorted = aux_draws.reshape(walk_size, chol_size, per_device, local_vectors)
     draws_sorted = draws_sorted.transpose(1, 0, 2, 3).reshape(total_walkers, local_vectors)
     field_sorted = draws_sorted - force_bias
@@ -37,27 +40,20 @@
         tiled=True,
     )
     operator = summed.reshape(group_walkers, slab_rows, orbitals)
-    start_terms = lax.all_gather(walkers.astype(jnp.bfloat16), "walk", axis=0, tiled=True)
-    taylor_term = jnp.einsum(
-        "wrs,wsi->wri", operator, start_terms, preferred_element_type=jnp.float32
-    )
-    summed_terms = taylor_term
-    for degree in range(2, 5):
-        term_low = taylor_term.astype(jnp.bfloat16)
+    operator = lax.all_to_all(operator, "walk", split_axis=0, concat_axis=1, tiled=True)
+    taylor_term = walkers
+    new_walkers = walkers
+    for degree in range(1, 5):
         taylor_term = (
             jnp.einsum(
                 "wrs,wsi->wri",
                 operator,
-                lax.all_gather(term_low, "walk", axis=1, tiled=True),
+                taylor_term.astype(jnp.bfloat16),
                 preferred_element_type=jnp.float32,
             )
             / degree
         )
-        summed_terms = summed_terms + taylor_term
-    returned = lax.all_to_all(
-        summed_terms.astype(jnp.bfloat16), "walk", split_axis=0, concat_axis=1, tiled=True
-    ).astype(summed_terms.dtype)
-    new_walkers = walkers + returned
+        new_walkers = new_walkers + taylor_term
     return (new_walkers, aux_field)
 
 

time: 676 us -> 334 us (0.49)
  waiting for transfers between devices: 585 us -> 202 us
  blocking collectives: 22.1 us -> 65.2 us
  matrix products: 28 us -> 16.9 us
  starting transfers between devices: 7.39 us -> 17.3 us
    all_gather x4 -> x0, waiting for transfers between devices: 249 us -> none  [the longest x3 183 us: body(): lax.all_gather(term_low, 'walk', axis=1, tiled=True)]
    psum x1 -> x0, waiting for transfers between devices: 148 us -> none  [body(): lax.psum(partial_bias.astype(jnp.bfloat16), 'walk').astype(jnp.float32)]
    all_gather x0 -> x1, blocking collectives: none -> 43.1 us  [body(): lax.all_gather(own_bias, 'walk', axis=0, tiled=True).astype(jnp.float32)]
    all_to_all x1 -> x2, waiting for transfers between devices: 9.9 us -> 25.3 us  [the longest x1 23.6 us: body(): lax.all_to_all(operator, 'walk', split_axis=0, concat_axis=1, tiled=True)]
    dot_general x4, matrix products: 12.6 us -> 2.29 us  [body(): jnp.einsum('wrs,wsi->wri', operator, taylor_term.astype(jnp.bfloat16), pr...]
    all_to_all x1 -> x2, starting transfers between devices: 7.1 us -> 17.2 us  [the longest x1 8.63 us: body(): lax.all_to_all(operator, 'walk', split_axis=0, concat_axis=1, tiled=True)]
  transfers between devices with their start and end apart: 8 -> 4, of which waited for: 8 -> 4; matrix products, arithmetic and copies ran while one was open for 2% -> 4% of each run, Pallas kernels for 0% -> 0%
where the time goes in v1:
time: 334 us
  waiting for transfers between devices  202 us (60%)
  blocking collectives  65.2 us (20%)
  starting transfers between devices  17.3 us (5%)
  matrix products  16.9 us (5%)
  local copies, waits for them, and re-layouts  16.8 us (5%)
  between operations  14.2 us (4%)
    reduce_scatter x1, waiting for transfers between devices, body(): lax.psum_scatter(jnp.dot(field_low, full_flat, preferred_element_type=jnp...  140 us
    all_gather x1, blocking collectives, body(): lax.all_gather(own_bias, 'walk', axis=0, tiled=True).astype(jnp.float32)  43.1 us
    all_gather x1, waiting for transfers between devices, body(): piece = lax.all_gather(green_slab, 'chol', axis=0, tiled=True)  36.7 us
    all_to_all x1, waiting for transfers between devices, body(): lax.all_to_all(operator, 'walk', split_axis=0, concat_axis=1, tiled=True)  23.6 us
    all_to_all x1, blocking collectives, body(): lax.all_to_all(green_half, 'walk', split_axis=1, concat_axis=0, tiled=True)  22.1 us
    unnamed x14, local copies, waits for them, and re-layouts  14.1 us
    dot_general x1, matrix products, body(): jnp.dot(field_low, full_flat, preferred_element_type=jnp.float32)  10.3 us
    all_to_all x1, starting transfers between devices, body(): lax.all_to_all(operator, 'walk', split_axis=0, concat_axis=1, tiled=True)  8.63 us
  transfers between devices with their start and end apart: 4, of which 4 were waited for; matrix products, arithmetic and copies ran while one was open for 4% of the time, Pallas kernels for 0%

profile of v1, /device:TPU:8, one launch (start us, length us, event | category | flops | bytes accessed | tf_op | source)
XLA Modules:
  0.0 333.9 jit_solution(10206859479181857573)
XLA Ops:
  7.2 0.0 copy-start
  7.2 0.0 all-gather.2.cloned.1.call-start
  7.2 1.5 fusion.7
  8.8 0.3 copy.41
  9.0 0.5 broadcast.6
  9.5 1.6 reduce.1
  11.2 22.1 %all_to_all.26 = bf16[16,2,2560]{2,1,0:T(2,128)(2,1)S(1)} all-to-all(bf16[16,2,2560]{2,1,0:T(2,128)(2,1)S(1)} %reshape.82), channel_id=1, replica_groups=mesh['walk'=16,'chol'=16] {'walk'}, dimensions={0} | all-to-all | bytes 327680 | tf_op jit(solution)/shard_map/all_to_all | solution.py:18
  33.3 0.1 reshape.83
  33.4 0.7 copy.26
  34.1 0.0 all-gather.2.cloned.1.call-update
  34.1 36.7 %all-gather.2.cloned.1.call-done = bf16[256,40,128]{2,0,1:T(8,128)(2,1)} async-done(((bf16[16,40,128]{2,0,1:T(8,128)(2,1)}), bf16[256,40,128]{2,0,1:T(8,128)(2,1)}) %all-gather.2.cloned.1.call-update) | async-done | bytes 2621456 | tf_op jit(solution)/shard_map/all_gather | solution.py:20
  70.9 2.7 fusion.8
  73.6 0.8 copy.28
  74.4 8.5 %all-to-all-start.1 = ((bf16[16,16,192]{2,1,0:T(8,128)(2,1)}), bf16[16,16,192]{2,1,0:T(8,128)(2,1)S(1)}, u32[]{:S(2)}, u32[]{:S(2)}) async-start(bf16[16,16,192]{2,1,0:T(8,128)(2,1)} %bitcast.7), calls=%async_computation.1 | async-start | bytes 262144 | tf_op jit(solution)/shard_map/all_to_all | solution.py:26
  83.0 0.0 reduce-scatter.2.cloned.1.call-start
  83.0 0.1 copy.23
  83.2 0.2 copy.24
  83.3 9.3 %copy.32 = bf16[24,8,40,640]{3,1,2,0:T(8,128)(2,1)} copy(bf16[24,8,40,640]{3,2,1,0:T(8,128)(2,1)} %bitcast.62) | data formatting | bytes 19660800
  92.6 1.7 all-to-all-done.1
  94.4 43.1 %all_gather.7 = bf16[256,192]{1,0:T(8,128)(2,1)S(1)} all-gather(bf16[16,192]{1,0:T(8,128)(2,1)S(1)} %reduce_sum.12), channel_id=1, replica_groups=mesh['walk'=16,'chol'=16] {'walk'}, dimensions={0}, use_global_device_ids=true | all-gather | bytes 104448 | tf_op jit(solution)/shard_map/all_gather | solution.py:28
  137.5 10.3 %convolution_convert_fusion = bf16[256,25600]{1,0:T(8,128)(2,1)} fusion(bf16[192,25600]{1,0:T(8,128)(2,1)} %bitcast.57, f32[256,192]{1,0:T(8,128)S(1)} %bitcast_subtract_fusion), kind=kOutput, calls=%fused_computation | convolution fusion | flops 2523185152 | bytes 23134208 | tf_op jit(solution)/shard_map/dot_general | solution.py:37
  147.9 0.0 reduce-scatter.2.cloned.1.call-update
  147.9 139.9 %reduce-scatter.2.cloned.1.call-done = bf16[16,25600]{1,0:T(8,128)(2,1)} async-done(((bf16[256,25600]{1,0:T(8,128)(2,1)}), bf16[16,25600]{1,0:T(8,128)(2,1)}) %reduce-scatter.2.cloned.1.call-update) | async-done | bytes 819216 | tf_op jit(solution)/shard_map/reduce_scatter | solution.py:36
  287.8 2.1 copy.33
  289.9 8.6 %all-to-all-start.2 = ((bf16[16,40,640]{2,1,0:T(8,128)(2,1)}), bf16[16,40,640]{2,1,0:T(8,128)(2,1)S(1)}, u32[]{:S(2)}, u32[]{:S(2)}) async-start(bf16[16,40,640]{2,1,0:T(8,128)(2,1)} %bitcast.63), calls=%async_computation.3 | async-start | bytes 1638400 | tf_op jit(solution)/shard_map/all_to_all | solution.py:43
  298.6 0.9 copy.29
  299.4 1.7 copy.30
  301.2 23.6 %all-to-all-done.2 = bf16[16,40,640]{2,1,0:T(8,128)(2,1)S(1)} async-done(((bf16[16,40,640]{2,1,0:T(8,128)(2,1)}), bf16[16,40,640]{2,1,0:T(8,128)(2,1)S(1)}, u32[]{:S(2)}, u32[]{:S(2)}) %all-to-all-start.2) | async-done | bytes 819232 | tf_op jit(solution)/shard_map/all_to_all | solution.py:43
  324.7 0.4 fusion.12
  325.1 0.4 convolution_multiply_fusion.2
  325.5 0.4 convolution_multiply_fusion.1
  325.9 1.1 fusion.3
  (9 shorter events, 0.1 us)
Async XLA Ops:
  7.2 63.7 %copy-start = (bf16[192,40,128]{2,1,0:T(8,128)(2,1)S(1)}, bf16[192,40,128]{2,1,0:T(8,128)(2,1)}, u32[]{:S(2)}) copy-start(bf16[192,40,128]{2,1,0:T(8,128)(2,1)} %param.8) | copy-start | bytes 5898244
  7.2 63.7 %all-gather.2.cloned.1.call-start = ((), (), s32[]{:S(2)}) async-start(), calls=%async_computation.4 | async-start | bytes 2785280 | tf_op jit(solution)/shard_map/all_gather | solution.py:20
  34.1 48.9 %copy-start.2 = (f32[256,192]{0,1:T(8,128)S(1)}, f32[256,192]{0,1:T(8,128)}, u32[]{:S(2)}) copy-start(f32[256,192]{0,1:T(8,128)} %param.7) | copy-start | bytes 589828
  74.4 19.9 %all-to-all-start.1 = ((bf16[16,16,192]{2,1,0:T(8,128)(2,1)}), bf16[16,16,192]{2,1,0:T(8,128)(2,1)S(1)}, u32[]{:S(2)}, u32[]{:S(2)}) async-start(bf16[16,16,192]{2,1,0:T(8,128)(2,1)} %bitcast.7), calls=%async_computation.1 | async-start | bytes 262144 | tf_op jit(solution)/shard_map/all_to_all | solution.py:26
  83.0 204.8 %reduce-scatter.2.cloned.1.call-start = ((), (), s32[]{:S(2)}) async-start(), calls=%async_computation.5 | async-start | bytes 13926400 | tf_op jit(solution)/shard_map/reduce_scatter | solution.py:36
  147.9 176.8 %copy-start.1 = (f32[1,640,128]{2,1,0:T(8,128)S(1)}, f32[1,640,128]{2,1,0:T(8,128)}, u32[]{:S(2)}) copy-start(f32[1,640,128]{2,1,0:T(8,128)} %param.5) | copy-start | bytes 983044
  289.9 34.8 %all-to-all-start.2 = ((bf16[16,40,640]{2,1,0:T(8,128)(2,1)}), bf16[16,40,640]{2,1,0:T(8,128)(2,1)S(1)}, u32[]{:S(2)}, u32[]{:S(2)}) async-start(bf16[16,40,640]{2,1,0:T(8,128)(2,1)} %bitcast.63), calls=%async_computation.3 | async-start | bytes 1638400 | tf_op jit(solution)/shard_map/all_to_all | solution.py:43
Sparse Core Ops, SparseCore 0:
  34.3 36.5 all-gather.1
  148.0 139.6 reduce-scatter.1

commit v2 on v1

v2 whole, which is shorter than its diff:
```python
import functools

import jax
import jax.numpy as jnp
from jax import lax
from jax.experimental import pallas as pl
from jax.experimental.pallas import tpu as pltpu
from jax.sharding import PartitionSpec as P

MESH = pl.DeviceIdType.MESH
BF16 = jnp.bfloat16
F32 = jnp.float32
ANY = pl.BlockSpec(memory_space=pl.ANY)
VMEM = pl.BlockSpec(memory_space=pltpu.VMEM)


def place():
    a = lax.axis_index("walk")
    b = lax.axis_index("chol")
    return a, b // 4, (b // 2) % 2, b % 2


def at(a, y, z, c):
    return (a, y * 4 + z * 2 + c)


def remote(src, dst, send, recv, target):
    return pltpu.make_async_remote_copy(
        src_ref=src, dst_ref=dst, send_sem=send, recv_sem=recv, device_id=target, device_id_type=MESH
    )


def greet(target):
    pl.semaphore_signal(pltpu.get_barrier_semaphore(), inc=1, device_id=target, device_id_type=MESH)


def field_kernel(
    walkers, inverse, draws, half, full,
    aux_out, field_out, ct_out,
    wv, iv, dv, hv, fv, gsend, g1, blocks, ht, ct, pb, bin_, ball, field,
    in_sem, ct_sem, ct_send, ct_recv, a_send, a_recv, g_send, g_recv, p_send, p_recv, b_send, b_recv,
    f_send, f_recv,
):
    a, y, z, c = place()
    up, down = (y + 1) % 4, (y + 3) % 4
    sibling = at(a, y, z, 1 - c)
    loads = [
        pltpu.make_async_copy(walkers, wv, in_sem.at[0]),
        pltpu.make_async_copy(inverse, iv, in_sem.at[1]),
        pltpu.make_async_copy(half, hv, in_sem.at[2]),
        pltpu.make_async_copy(full, fv, in_sem.at[3]),
        pltpu.make_async_copy(draws, dv, in_sem.at[4]),
    ]
    for load in loads:
        load.start()

    def greet_walk(d, _):
        greet(at((a + d) % 16, y, z, c))
        return 0

    lax.fori_loop(1, 16, greet_walk, 0)
    greet(at(a, up, z, c))
    greet(at(a, down, z, c))
    greet(at(a, y, 1 - z, c))
    greet(sibling)

    loads[0].wait()
    loads[1].wait()
    green = jnp.dot(
        wv[0], iv[0], precision=lax.Precision.HIGHEST, preferred_element_type=F32
    ).astype(BF16)
    gsend[...] = green.reshape(16, 40, 128)
    pl.semaphore_wait(pltpu.get_barrier_semaphore(), 19)

    def green_copy(d):
        to = (a + d) % 16
        return remote(gsend.at[to], g1.at[a], a_send.at[d], a_recv.at[d], at(to, y, z, c))

    def start_green(d, _):
        green_copy(d).start()
        return 0

    lax.fori_loop(1, 16, start_green, 0)
    g1[a] = gsend[a]

    loads[2].wait()

    def turn_half(i, _):
        n0 = pl.multiple_of(i * 16, 16)
        ht[:, pl.ds(n0, 16), :] = jnp.swapaxes(hv[pl.ds(n0, 16)], 0, 1)
        return 0

    lax.fori_loop(0, 12, turn_half, 0)

    def wait_green(d, _):
        green_copy(d).wait()
        return 0

    lax.fori_loop(1, 16, wait_green, 0)

    def slot(yy, zz):
        return c * 8 + yy * 2 + zz

    own = slot(y, z)
    blocks[own] = jnp.swapaxes(g1[...], 0, 1)

    first, second = pl.ds(0, 20), pl.ds(20, 20)

    def spread(index, ref, target):
        return remote(ref, ref, g_send.at[index], g_recv.at[index], target)

    to_up, to_down, to_z = at(a, up, z, c), at(a, down, z, c), at(a, y, 1 - z, c)
    far = (y + 2) % 4
    block = lambda yy, zz: blocks.at[slot(yy, zz)]
    copies = [
        spread(0, block(y, z), to_up),
        spread(1, block(y, z), to_down),
        spread(2, block(y, z), to_z),
        spread(3, block(y, z), sibling),
        spread(4, block(y, 1 - z), to_up),
        spread(5, block(y, 1 - z), to_down),
        spread(6, block(y, 1 - z), sibling),
        spread(7, block(down, z).at[first], to_up),
        spread(8, block(down, z), sibling),
        spread(9, block(up, z).at[second], to_down),
        spread(10, block(up, z), sibling),
        spread(11, block(down, 1 - z).at[first], to_up),
        spread(12, block(down, 1 - z), sibling),
        spread(13, block(up, 1 - z).at[second], to_down),
        spread(14, block(up, 1 - z), sibling),
        spread(15, block(far, z), sibling),
        spread(16, block(far, 1 - z), sibling),
    ]
    for index in (0, 1, 2, 3):
        copies[index].start()

    loads[3].wait()

    def turn_full(group):
        def turn(i, _):
            n0 = pl.multiple_of(i * 16, 16)
            ct[group, :, pl.ds(n0, 16), :] = jnp.swapaxes(
                fv[pl.ds(n0, 16), group * 8 : group * 8 + 8, :], 0, 1
            )
            return 0

        lax.fori_loop(0, 12, turn, 0)

    def keep(i):
        group = 4 if i == 2 else 2 * c + i
        return pltpu.make_async_copy(ct.at[group], ct_out.at[i, :, c], ct_sem.at[i])

    def give(i):
        group = 4 if i == 2 else 2 * (1 - c) + i
        return remote(ct.at[group], ct_out.at[i, :, c], ct_send.at[i], ct_recv.at[i], sibling)

    turn_full(0)
    turn_full(1)
    copies[2].wait_recv()
    for index in (4, 5, 6):
        copies[index].start()
    copies[0].wait_recv()
    copies[1].wait_recv()
    for index in (7, 9, 8, 10):
        copies[index].start()
    turn_full(2)
    turn_full(3)
    for i in (0, 1):
        keep(i).start()
        give(i).start()
    copies[4].wait_recv()
    copies[5].wait_recv()
    for index in (11, 13, 12, 14):
        copies[index].start()
    turn_full(4)
    keep(2).start()
    give(2).start()
    copies[7].wait_recv()
    copies[9].wait_recv()
    copies[15].start()
    copies[11].wait_recv()
    copies[13].wait_recv()
    copies[16].start()
    loads[4].wait()
    draws_by_slot = jnp.swapaxes(dv[...], 0, 1).reshape(8, 2, 16, 192)
    for index in (3, 6, 8, 10, 12, 14, 15, 16):
        copies[index].wait_recv()

    def bias_step(i, acc):
        p0 = i * 8
        left = jnp.concatenate([blocks[:, p0 + q].reshape(256, 128) for q in range(8)], axis=1)
        right = jnp.concatenate([ht[p0 + q] for q in range(8)], axis=1)
        return acc + lax.dot_general(
            left, right, (((1,), (1,)), ((), ())), preferred_element_type=F32
        )

    partial = lax.fori_loop(0, 5, bias_step, jnp.zeros((256, 192), F32))
    pb[...] = partial.astype(BF16).reshape(16, 16, 192)

    def part_copy(d):
        to = (a + d) % 16
        return remote(pb.at[to], bin_.at[a], p_send.at[d], p_recv.at[d], at(to, y, z, c))

    def start_part(d, _):
        part_copy(d).start()
        return 0

    def wait_part(d, _):
        part_copy(d).wait()
        return 0

    lax.fori_loop(1, 16, start_part, 0)
    bin_[a] = pb[a]
    lax.fori_loop(1, 16, wait_part, 0)
    ball[a] = jnp.sum(bin_[...].astype(F32), axis=0).astype(BF16)

    def bias_copy(d):
        to = (a + d) % 16
        return remote(ball.at[a], ball.at[a], b_send.at[d], b_recv.at[d], at(to, y, z, c))

    def bias_from(d):
        there = (a + 16 - d) % 16
        return remote(ball.at[there], ball.at[there], b_send.at[d], b_recv.at[d], at(there, y, z, c))

    def start_bias(d, _):
        bias_copy(d).start()
        return 0

    def wait_bias(d, _):
        bias_copy(d).wait_send()
        bias_from(d).wait_recv()
        return 0

    lax.fori_loop(1, 16, start_bias, 0)
    lax.fori_loop(1, 16, wait_bias, 0)
    bias = jnp.swapaxes(ball[...].astype(F32).reshape(2, 8, 16, 192), 0, 1)
    shifted = draws_by_slot - bias
    for owner in range(2):
        field[c, owner] = shifted[:, owner].astype(BF16)
    field_copy = remote(field.at[c], field.at[c], f_send, f_recv, sibling)
    field_copy.start()
    aux_out[...] = jnp.swapaxes(shifted.reshape(16, 16, 192), 0, 1)
    for copy in copies:
        copy.wait_send()
    for i in range(3):
        keep(i).wait()
        give(i).wait()
    field_copy.wait()
    field_out[...] = field[...]


def propagate_kernel(
    walkers, field, ct_in,
    out,
    ct, part, pass_up, pass_down, from_down, from_up, z_out, from_z, turned, operator,
    ct_sem, s_up, r_up, s_down, r_down, z_send, z_recv, o_send, o_recv,
):
    a, y, z, c = place()
    up, down, far = (y + 1) % 4, (y + 3) % 4, (y + 2) % 4
    to_up, to_down, to_z = at(a, up, z, c), at(a, down, z, c), at(a, y, 1 - z, c)
    loads = [pltpu.make_async_copy(ct_in.at[i], ct.at[i], ct_sem.at[i]) for i in range(3)]
    for load in loads:
        load.start()

    def greet_walk(d, _):
        greet(at((a + d) % 16, y, z, c))
        greet(at((a + d) % 16, y, z, 1 - c))
        return 0

    lax.fori_loop(1, 16, greet_walk, 0)
    greet(to_up)
    greet(to_down)
    greet(to_z)
    greet(at(a, y, z, 1 - c))

    low, high = pl.ds(0, 4), pl.ds(4, 4)

    def owner_of(k):
        return c if k == 4 else k % 2

    def group_of(k):
        return 4 if k == 4 else 2 * c + k // 2

    def multiply(k):
        if k % 2 == 0:
            loads[k // 2].wait()
        owner = owner_of(k)
        left = [field[s, owner].reshape(128, 192) for s in range(2)]

        def row(r, _):
            value = jnp.dot(left[0], ct[k // 2, r, 0], preferred_element_type=F32)
            value = value + jnp.dot(left[1], ct[k // 2, r, 1], preferred_element_type=F32)
            part[k, :, :, r] = value.astype(BF16).reshape(4, 2, 16, 640)
            return 0

        lax.fori_loop(0, 8, row, 0)

    def sends(k):
        return (
            remote(part.at[k, far, :, low], pass_up.at[k], s_up.at[k, 0], r_up.at[k, 0], to_up),
            remote(part.at[k, far, :, high], pass_down.at[k], s_down.at[k, 0], r_down.at[k, 0], to_down),
            remote(part.at[k, up, :, high], from_down.at[k, :, high], s_up.at[k, 1], r_up.at[k, 1], to_up),
            remote(part.at[k, down, :, low], from_up.at[k, :, low], s_down.at[k, 1], r_down.at[k, 1], to_down),
            remote(pass_up.at[k], from_down.at[k, :, low], s_up.at[k, 2], r_up.at[k, 2], to_up),
            remote(pass_down.at[k], from_up.at[k, :, high], s_down.at[k, 2], r_down.at[k, 2], to_down),
        )

    def begin(k):
        for copy in sends(k)[:4]:
            copy.start()

    def pass_on(k):
        copies = sends(k)
        copies[0].wait_recv()
        pass_up[k] = (pass_up[k].astype(F32) + part[k, up, :, 0:4].astype(F32)).astype(BF16)
        copies[4].start()
        copies[1].wait_recv()
        pass_down[k] = (pass_down[k].astype(F32) + part[k, down, :, 4:8].astype(F32)).astype(BF16)
        copies[5].start()

    def z_copy(k):
        return remote(z_out.at[k], from_z.at[k], z_send.at[k], z_recv.at[k], to_z)

    def over_z(k):
        for copy in sends(k)[2:]:
            copy.wait_recv()
        other = 1 - z
        total = part[k, y, other].astype(F32) + from_down[k, other].astype(F32)
        z_out[k] = (total + from_up[k, other].astype(F32)).astype(BF16)
        z_copy(k).start()

    def owner_copy(k, d):
        to = (a + d) % 16
        return remote(
            turned.at[k, to], operator.at[a, group_of(k)],
            o_send.at[k, d], o_recv.at[group_of(k), d], at(to, y, z, owner_of(k)),
        )

    def deliver(k):
        z_copy(k).wait_recv()
        total = part[k, y, z].astype(F32) + from_down[k, z].astype(F32)
        total = total + from_up[k, z].astype(F32) + from_z[k].astype(F32)
        turned[k] = jnp.swapaxes(total, 0, 1).astype(BF16)

        def start(d, _):
            owner_copy(k, d).start()
            return 0

        lax.fori_loop(1, 16, start, 0)
        if k == 4:
            operator[a, 4] = turned[k, a]
        else:

            @pl.when(c == k % 2)
            def _():
                operator[a, group_of(k)] = turned[k, a]

            @pl.when(c != k % 2)
            def _():
                owner_copy(k, 0).start()

    multiply(0)
    pl.semaphore_wait(pltpu.get_barrier_semaphore(), 34)
    begin(0)
    multiply(1)
    begin(1)
    for k in range(5):
        pass_on(k)
        if k + 2 < 5:
            multiply(k + 2)
            begin(k + 2)
        if k >= 1:
            over_z(k - 1)
        if k >= 2:
            deliver(k - 2)
    over_z(4)
    deliver(3)
    deliver(4)

    def arrival(group, d):
        return remote(
            turned.at[0, 0], operator.at[0, group], o_send.at[0, 0], o_recv.at[group, d], at(a, y, z, 1 - c)
        )

    for group in range(5):

        def wait_for(d, _, group=group):
            arrival(group, d).wait_recv()
            return 0

        lax.fori_loop(1, 16, wait_for, 0)
        if group < 4:

            @pl.when(c != group // 2)
            def _(group=group):
                arrival(group, 0).wait_recv()

    matrix = operator[...].reshape(640, 640)
    term = walkers[0]
    total = term
    for degree in range(1, 5):
        term = jnp.dot(matrix, term.astype(BF16), preferred_element_type=F32) * (1.0 / degree)
        total = total + term
    out[0] = total

    for k in range(5):
        for copy in sends(k):
            copy.wait_send()
        z_copy(k).wait_send()

        def wait_sent(d, _, k=k):
            owner_copy(k, d).wait_send()
            return 0

        lax.fori_loop(1, 16, wait_sent, 0)
        if k < 4:

            @pl.when(c != k % 2)
            def _(k=k):
                owner_copy(k, 0).wait_send()


def shape(*dims, dtype=BF16):
    return jax.ShapeDtypeStruct(dims, dtype)


def dma(*dims):
    return pltpu.SemaphoreType.DMA(dims)


def body(walkers, intersection_inverse, aux_draws, chol_half, chol_full):
    aux, field, ct = pl.pallas_call(
        field_kernel,
        out_shape=(
            shape(16, 16, 192, dtype=F32),
            shape(2, 2, 8, 16, 192),
            shape(3, 8, 2, 192, 640),
        ),
        in_specs=[ANY] * 5,
        out_specs=(VMEM, VMEM, ANY),
        scratch_shapes=[
            pltpu.VMEM((1, 640, 128), F32),
            pltpu.VMEM((1, 128, 128), F32),
            pltpu.VMEM((16, 16, 192), F32),
            pltpu.VMEM((192, 40, 128), BF16),
            pltpu.VMEM((192, 40, 640), BF16),
            pltpu.VMEM((16, 40, 128), BF16),
            pltpu.VMEM((16, 40, 128), BF16),
            pltpu.VMEM((16, 40, 16, 128), BF16),
            pltpu.VMEM((40, 192, 128), BF16),
            pltpu.VMEM((5, 8, 192, 640), BF16),
            pltpu.VMEM((16, 16, 192), BF16),
            pltpu.VMEM((16, 16, 192), BF16),
            pltpu.VMEM((16, 16, 192), BF16),
            pltpu.VMEM((2, 2, 8, 16, 192), BF16),
            dma(5), dma(3), dma(3), dma(3), dma(16), dma(16), dma(17), dma(17),
            dma(16), dma(16), dma(16), dma(16), dma(), dma(),
        ],
        compiler_params=pltpu.CompilerParams(
            collective_id=0, has_side_effects=True, vmem_limit_bytes=56 * 2**20
        ),
        name="field",
    )(walkers, intersection_inverse, aux_draws.reshape(16, 16, 192), chol_half, chol_full)
    new_walkers = pl.pallas_call(
        propagate_kernel,
        out_shape=shape(1, 640, 128, dtype=F32),
        in_specs=[VMEM, VMEM, ANY],
        out_specs=VMEM,
        scratch_shapes=[
            pltpu.VMEM((3, 8, 2, 192, 640), BF16),
            pltpu.VMEM((5, 4, 2, 8, 16, 640), BF16),
            pltpu.VMEM((5, 2, 4, 16, 640), BF16),
            pltpu.VMEM((5, 2, 4, 16, 640), BF16),
            pltpu.VMEM((5, 2, 8, 16, 640), BF16),
            pltpu.VMEM((5, 2, 8, 16, 640), BF16),
            pltpu.VMEM((5, 8, 16, 640), BF16),
            pltpu.VMEM((5, 8, 16, 640), BF16),
            pltpu.VMEM((5, 16, 8, 640), BF16),
            pltpu.VMEM((16, 5, 8, 640), BF16),
            dma(3), dma(5, 3), dma(5, 3), dma(5, 3), dma(5, 3), dma(5), dma(5), dma(5, 16), dma(5, 16),
        ],
        compiler_params=pltpu.CompilerParams(
            collective_id=1, has_side_effects=True, vmem_limit_bytes=56 * 2**20
        ),
        name="propagate",
    )(walkers, field, ct)
    return new_walkers, aux.reshape(256, 192)


def solution(mesh):
    placed = (
        P(("walk", "chol"), None, None),
        P(("walk", "chol"), None, None),
        P(None, "chol"),
        P("chol", "walk", None),
        P("chol", "walk", None),
    )
    return jax.shard_map(
        body,
        mesh=mesh,
        in_specs=placed,
        out_specs=(P(("walk", "chol"), None, None), P(None, "chol")),
        check_vma=False,
    )
```

time: 334 us -> 140 us (0.42)
  waiting for transfers between devices: 202 us -> 0 us
  Pallas kernels: 0 us -> 132 us
  blocking collectives: 65.2 us -> 0 us
  starting transfers between devices: 17.3 us -> 0 us
  matrix products: 16.9 us -> 0 us
  between operations: 14.2 us -> 0.66 us
  local copies, waits for them, and re-layouts: 16.8 us -> 4.28 us
    reduce_scatter x1 -> x0, waiting for transfers between devices: 140 us -> none  [body(): lax.psum_scatter(jnp.dot(field_low, full_flat, preferred_element_type=jnp...]
    pallas_call x0 -> x2, Pallas kernels: none -> 132 us  [the longest x1 82.2 us: body(): pl.pallas_call(propagate_kernel, out_shape=shape(1, 640, 128, dtype=F32),...]
    all_gather x1 -> x0, blocking collectives: 43.1 us -> none  [body(): lax.all_gather(own_bias, 'walk', axis=0, tiled=True).astype(jnp.float32)]
    all_gather x1 -> x0, waiting for transfers between devices: 36.7 us -> none  [body(): piece = lax.all_gather(green_slab, 'chol', axis=0, tiled=True)]
    all_to_all x2 -> x0, waiting for transfers between devices: 25.3 us -> none  [the longest x1 23.6 us: body(): lax.all_to_all(operator, 'walk', split_axis=0, concat_axis=1, tiled=True)]
    all_to_all x1 -> x0, blocking collectives: 22.1 us -> none  [body(): lax.all_to_all(green_half, 'walk', split_axis=1, concat_axis=0, tiled=True)]
    all_to_all x2 -> x0, starting transfers between devices: 17.2 us -> none  [the longest x1 8.63 us: body(): lax.all_to_all(operator, 'walk', split_axis=0, concat_axis=1, tiled=True)]
    dot_general x7 -> x0, matrix products: 16.9 us -> none  [the longest x1 10.3 us: body(): jnp.dot(field_low, full_flat, preferred_element_type=jnp.float32)]
  transfers between devices with their start and end apart: 4 -> 0, of which waited for: 4 -> 0; matrix products, arithmetic and copies ran while one was open for 4% -> 0% of each run, Pallas kernels for 0% -> 0%
where the time goes in v2:
time: 140 us; the launch traced here: 137 us
  Pallas kernels  132 us (94%)
  local copies, waits for them, and re-layouts  4.28 us (3%)
    pallas_call x1, Pallas kernels, body(): pl.pallas_call(propagate_kernel, out_shape=shape(1, 640, 128, dtype=F32),...  82.2 us
    pallas_call x1, Pallas kernels, body(): pl.pallas_call(field_kernel, out_shape=(shape(16, 16, 192, dtype=F32), sh...  50.1 us
    unnamed x5, local copies, waits for them, and re-layouts  4.28 us

profile of v2, /device:TPU:8, one launch (start us, length us, event | category | flops | bytes accessed | tf_op | source)
XLA Modules:
  0.0 137.2 jit_solution(7343379104833648475)
XLA Ops:
  0.6 1.8 %copy.7 = f32[256,192]{1,0:T(8,128)} copy(f32[256,192]{0,1:T(8,128)} %param.7) | data formatting | bytes 393216 | tf_op args[2]
  2.4 50.1 %field.1 = (f32[16,16,192]{2,1,0:T(8,128)}, bf16[2,2,8,16,192]{4,3,2,1,0:T(8,128)(2,1)}, bf16[3,8,2,192,640]{4,3,2,1,0:T(8,128)(2,1)}) custom-call(f32[1,640,128]{2,1,0:T(8,128)} %walkers.3, f32[1,128,128]{2,1,0:T(8,128)} %inverse.1, f32[16,16,192]{2,1,0:T(8,128)} %bitcast.2, bf16[192,40,128]{2,1,0:T(8,128)(2,1)} %half.1, bf16[192,40,640]{2,1,0:T(8,128)(2,1)} %full.1), custom_call_target="tpu_custom_call" | custom-call | tf_op jit(solution)/shard_map/field/pallas_call | solution.py:432
  52.5 0.0 copy-start
  52.5 82.2 %propagate.1 = f32[1,640,128]{2,1,0:T(8,128)} custom-call(f32[1,640,128]{2,1,0:T(8,128)} %walkers.3, bf16[2,2,8,16,192]{4,3,2,1,0:T(8,128)(2,1)} %get-tuple-element.5.field, bf16[3,8,2,192,640]{4,3,2,1,0:T(8,128)(2,1)} %get-tuple-element.6.ct_in), custom_call_target="tpu_custom_call" | custom-call | tf_op jit(solution)/shard_map/propagate/pallas_call | solution.py:464
  134.7 0.0 copy-done
  134.7 0.8 copy.8
  135.5 1.7 %copy.10 = f32[1,640,128]{2,1,0:T(8,128)} copy(f32[1,640,128]{2,1,0:T(8,128)} %propagate.1) | data formatting | bytes 655360
Async XLA Ops:
  52.5 82.3 %copy-start = (f32[16,16,192]{2,1,0:T(8,128)S(1)}, f32[16,16,192]{2,1,0:T(8,128)}, u32[]{:S(2)}) copy-start(f32[16,16,192]{2,1,0:T(8,128)} %get-tuple-element.7) | copy-start | bytes 589828

commit v3 on v1

v3 whole, which is shorter than its diff:
```python
import jax
import jax.numpy as jnp
from jax import lax
from jax.experimental import pallas as pl
from jax.experimental.pallas import tpu as pltpu
from jax.sharding import PartitionSpec as P

MESH = pl.DeviceIdType.MESH
BF16 = jnp.bfloat16
F32 = jnp.float32
ANY = pl.BlockSpec(memory_space=pl.ANY)
VMEM = pl.BlockSpec(memory_space=pltpu.VMEM)


def place():
    a = lax.axis_index("walk")
    b = lax.axis_index("chol")
    return a, b // 4, (b // 2) % 2, b % 2


def at(a, y, z, c):
    return (a, y * 4 + z * 2 + c)


def remote(src, dst, send, recv, target):
    return pltpu.make_async_remote_copy(
        src_ref=src, dst_ref=dst, send_sem=send, recv_sem=recv, device_id=target, device_id_type=MESH
    )


def greet(target):
    pl.semaphore_signal(pltpu.get_barrier_semaphore(), inc=1, device_id=target, device_id_type=MESH)


def kernel(
    walkers, inverse, draws, half, full,
    out, aux_out,
    wv, iv, dv, hv, fv, gsend, g1, blocks, ht, ct, given, pb, parts_in, ball, field,
    part, pass_up, pass_down, from_down, from_up, z_out, from_z,
    zin, zsum, z_pass_up, z_pass_down, z_from_down, z_from_up, turned, operator,
    in_sem, ct_send, ct_recv, a_send, a_recv, g_send, g_recv, p_send, p_recv, b_send, b_recv,
    f_send, f_recv, s_up, r_up, s_down, r_down, z_send, z_recv, o_send, o_recv,
):
    a, y, z, c = place()
    up, down, far = (y + 1) % 4, (y + 3) % 4, (y + 2) % 4
    to_up, to_down, to_z = at(a, up, z, c), at(a, down, z, c), at(a, y, 1 - z, c)
    sibling = at(a, y, z, 1 - c)

    def load(index):
        pair = ((walkers, wv), (inverse, iv), (half, hv), (full, fv), (draws, dv))[index]
        return pltpu.make_async_copy(pair[0], pair[1], in_sem.at[index])

    for index in range(5):
        load(index).start()

    def greet_walk(d, _):
        greet(at((a + d) % 16, y, z, c))
        greet(at((a + d) % 16, y, z, 1 - c))
        return 0

    lax.fori_loop(1, 16, greet_walk, 0)
    for target in (to_up, to_down, to_z, sibling):
        greet(target)

    load(0).wait()
    load(1).wait()
    green = jnp.dot(
        wv[0], iv[0], precision=lax.Precision.HIGHEST, preferred_element_type=F32
    ).astype(BF16)
    gsend[...] = green.reshape(16, 40, 128)
    pl.semaphore_wait(pltpu.get_barrier_semaphore(), 34)

    def each_other(step):
        def run(d, _):
            step(d)
            return 0

        lax.fori_loop(1, 16, run, 0)

    def peer(d):
        return (a + d) % 16

    def green_copy(d):
        return remote(
            gsend.at[peer(d)], g1.at[a], a_send.at[d], a_recv.at[d], at(peer(d), y, z, c)
        )

    each_other(lambda d: green_copy(d).start())
    g1[a] = gsend[a]

    load(2).wait()

    def turn_half(i, _):
        n0 = pl.multiple_of(i * 16, 16)
        ht[:, pl.ds(n0, 16), :] = jnp.swapaxes(hv[pl.ds(n0, 16)], 0, 1)
        return 0

    lax.fori_loop(0, 12, turn_half, 0)

    load(3).wait()

    def turn_full(group, target):
        def turn(i, _):
            n0 = pl.multiple_of(i * 16, 16)
            target[:, pl.ds(n0, 16), :] = jnp.swapaxes(
                fv[pl.ds(n0, 16), group * 8 : group * 8 + 8, :], 0, 1
            )
            return 0

        lax.fori_loop(0, 12, turn, 0)

    def turn_given(i):
        for core in range(2):

            @pl.when(c == core)
            def _(core=core):
                turn_full(2 * (1 - core) + i, given.at[i])

    def turn_kept(i):
        for core in range(2):

            @pl.when(c == core)
            def _(core=core):
                turn_full(2 * core + i, ct.at[i, :, core])

    def give(i):
        source = ct.at[2, :, c] if i == 2 else given.at[i]
        return remote(source, ct.at[i, :, c], ct_send.at[i], ct_recv.at[i], sibling)

    turn_given(0)
    give(0).start()

    each_other(lambda d: green_copy(d).wait())

    def slot(yy, zz):
        return c * 8 + yy * 2 + zz

    own = slot(y, z)
    blocks[own] = jnp.swapaxes(g1[...], 0, 1)
    first, second = pl.ds(0, 20), pl.ds(20, 20)

    def spread(index):
        yy, zz, rows, target = (
            (y, z, None, to_up),
            (y, z, None, to_down),
            (y, z, None, to_z),
            (y, z, None, sibling),
            (y, 1 - z, None, to_up),
            (y, 1 - z, None, to_down),
            (y, 1 - z, None, sibling),
            (down, z, first, to_up),
            (down, z, None, sibling),
            (up, z, second, to_down),
            (up, z, None, sibling),
            (down, 1 - z, first, to_up),
            (down, 1 - z, None, sibling),
            (up, 1 - z, second, to_down),
            (up, 1 - z, None, sibling),
            (far, z, None, sibling),
            (far, 1 - z, None, sibling),
        )[index]
        ref = blocks.at[slot(yy, zz)]
        ref = ref if rows is None else ref.at[rows]
        return remote(ref, ref, g_send.at[index], g_recv.at[index], target)

    for index in (0, 1, 2, 3):
        spread(index).start()
    turn_given(1)
    give(1).start()

    @pl.when(c == 0)
    def _():
        turn_full(4, ct.at[2, :, 0])

    @pl.when(c == 1)
    def _():
        turn_full(4, ct.at[2, :, 1])

    spread(2).wait_recv()
    for index in (4, 5, 6):
        spread(index).start()
    spread(0).wait_recv()
    spread(1).wait_recv()
    for index in (7, 9, 8, 10):
        spread(index).start()
    give(2).start()
    turn_kept(0)
    spread(4).wait_recv()
    spread(5).wait_recv()
    for index in (11, 13, 12, 14):
        spread(index).start()
    turn_kept(1)
    load(4).wait()
    draws_by_slot = jnp.swapaxes(dv[...].T.reshape(16, 16, 192), 0, 1).reshape(8, 2, 16, 192)
    spread(7).wait_recv()
    spread(9).wait_recv()
    spread(15).start()
    spread(11).wait_recv()
    spread(13).wait_recv()
    spread(16).start()
    for index in (3, 6, 8, 10, 12, 14, 15, 16):
        spread(index).wait_recv()

    def bias_step(i, acc):
        p0 = i * 8
        left = jnp.concatenate([blocks[:, p0 + q].reshape(256, 128) for q in range(8)], axis=1)
        right = jnp.concatenate([ht[p0 + q] for q in range(8)], axis=1)
        return acc + lax.dot_general(
            left, right, (((1,), (1,)), ((), ())), preferred_element_type=F32
        )

    partial = lax.fori_loop(0, 5, bias_step, jnp.zeros((256, 192), F32))
    pb[...] = partial.astype(BF16).reshape(16, 16, 192)

    def part_copy(d):
        return remote(
            pb.at[peer(d)], parts_in.at[a], p_send.at[d], p_recv.at[d], at(peer(d), y, z, c)
        )

    each_other(lambda d: part_copy(d).start())
    parts_in[a] = pb[a]
    each_other(lambda d: part_copy(d).wait_recv())
    ball[a] = jnp.sum(parts_in[...].astype(F32), axis=0).astype(BF16)

    def bias_copy(d):
        return remote(ball.at[a], ball.at[a], b_send.at[d], b_recv.at[d], at(peer(d), y, z, c))

    def bias_from(d):
        there = ball.at[peer(16 - d)]
        return remote(there, there, b_send.at[d], b_recv.at[d], at(peer(16 - d), y, z, c))

    each_other(lambda d: bias_copy(d).start())
    each_other(lambda d: bias_from(d).wait_recv())
    bias = jnp.swapaxes(ball[...].astype(F32).reshape(2, 8, 16, 192), 0, 1)
    shifted = draws_by_slot - bias
    for owner in range(2):
        field[c, owner] = shifted[:, owner].astype(BF16)
    field_copy = remote(field.at[c], field.at[c], f_send, f_recv, sibling)
    field_copy.start()
    for i in range(3):
        give(i).wait_recv()
    field_copy.wait_recv()

    low, high = pl.ds(0, 4), pl.ds(4, 4)

    def owner_of(k):
        return c if k == 4 else k % 2

    def group_of(k):
        return 4 if k == 4 else 2 * c + k // 2

    def multiply(k):
        owner = owner_of(k)
        left = [field[s, owner].reshape(128, 192) for s in range(2)]

        def row(r, _):
            value = jnp.dot(left[0], ct[k // 2, r, 0], preferred_element_type=F32)
            value = value + jnp.dot(left[1], ct[k // 2, r, 1], preferred_element_type=F32)
            part[k, :, :, r] = value.astype(BF16).reshape(4, 2, 16, 640)
            return 0

        lax.fori_loop(0, 8, row, 0)

    def send_up(k, step):
        if k == 4:
            pair = (
                (zsum.at[far, low], z_pass_up),
                (zsum.at[up, high], z_from_down.at[high]),
                (z_pass_up, z_from_down.at[low]),
            )[step]
        else:
            pair = (
                (part.at[k, far, :, low], pass_up.at[k]),
                (part.at[k, up, :, high], from_down.at[k, :, high]),
                (pass_up.at[k], from_down.at[k, :, low]),
            )[step]
        return remote(pair[0], pair[1], s_up.at[k, step], r_up.at[k, step], to_up)

    def send_down(k, step):
        if k == 4:
            pair = (
                (zsum.at[far, high], z_pass_down),
                (zsum.at[down, low], z_from_up.at[low]),
                (z_pass_down, z_from_up.at[high]),
            )[step]
        else:
            pair = (
                (part.at[k, far, :, high], pass_down.at[k]),
                (part.at[k, down, :, low], from_up.at[k, :, low]),
                (pass_down.at[k], from_up.at[k, :, high]),
            )[step]
        return remote(pair[0], pair[1], s_down.at[k, step], r_down.at[k, step], to_down)

    def begin(k):
        for step in range(2):
            send_up(k, step).start()
            send_down(k, step).start()

    def pass_on(k):
        send_up(k, 0).wait_recv()
        if k == 4:
            z_pass_up[...] = (z_pass_up[...].astype(F32) + zsum[up, 0:4].astype(F32)).astype(BF16)
        else:
            pass_up[k] = (pass_up[k].astype(F32) + part[k, up, :, 0:4].astype(F32)).astype(BF16)
        send_up(k, 2).start()
        send_down(k, 0).wait_recv()
        if k == 4:
            z_pass_down[...] = (
                z_pass_down[...].astype(F32) + zsum[down, 4:8].astype(F32)
            ).astype(BF16)
        else:
            pass_down[k] = (
                pass_down[k].astype(F32) + part[k, down, :, 4:8].astype(F32)
            ).astype(BF16)
        send_down(k, 2).start()

    def gathered(k):
        for step in (1, 2):
            send_up(k, step).wait_recv()
            send_down(k, step).wait_recv()

    def z_copy(k):
        if k == 4:
            return remote(part.at[4, :, 1 - z], zin, z_send.at[4], z_recv.at[4], to_z)
        return remote(z_out.at[k], from_z.at[k], z_send.at[k], z_recv.at[k], to_z)

    def over_z(k):
        gathered(k)
        other = 1 - z
        total = part[k, y, other].astype(F32) + from_down[k, other].astype(F32)
        z_out[k] = (total + from_up[k, other].astype(F32)).astype(BF16)
        z_copy(k).start()

    def owner_copy(k, d):
        return remote(
            turned.at[k, peer(d)], operator.at[a, group_of(k)],
            o_send.at[k, d], o_recv.at[group_of(k), d], at(peer(d), y, z, owner_of(k)),
        )

    def deliver(k):
        if k == 4:
            gathered(4)
            total = zsum[y].astype(F32) + z_from_down[...].astype(F32)
            total = total + z_from_up[...].astype(F32)
        else:
            z_copy(k).wait_recv()
            total = part[k, y, z].astype(F32) + from_down[k, z].astype(F32)
            total = total + from_up[k, z].astype(F32) + from_z[k].astype(F32)
        turned[k] = jnp.swapaxes(total, 0, 1).astype(BF16)
        each_other(lambda d: owner_copy(k, d).start())
        if k == 4:
            operator[a, 4] = turned[k, a]
        else:

            @pl.when(c == k % 2)
            def _():
                operator[a, group_of(k)] = turned[k, a]

            @pl.when(c != k % 2)
            def _():
                owner_copy(k, 0).start()

    multiply(0)
    begin(0)
    multiply(4)
    z_copy(4).start()
    multiply(1)
    begin(1)
    aux_out[...] = jnp.swapaxes(shifted.reshape(16, 16, 192), 0, 1).reshape(256, 192).T
    multiply(2)
    pass_on(0)
    begin(2)
    multiply(3)
    pass_on(1)
    begin(3)
    over_z(0)
    z_copy(4).wait_recv()
    zsum[...] = (part[4, :, z].astype(F32) + zin[...].astype(F32)).astype(BF16)
    pass_on(2)
    deliver(0)
    over_z(1)
    pass_on(3)
    begin(4)
    deliver(1)
    over_z(2)
    over_z(3)
    pass_on(4)
    deliver(2)
    deliver(3)
    deliver(4)

    each_other(lambda d: part_copy(d).wait_send())
    each_other(lambda d: bias_copy(d).wait_send())
    for index in range(17):
        spread(index).wait_send()
    for i in range(3):
        give(i).wait_send()
    field_copy.wait_send()
    for k in range(5):
        for step in range(3):
            send_up(k, step).wait_send()
            send_down(k, step).wait_send()
        z_copy(k).wait_send()
        each_other(lambda d, k=k: owner_copy(k, d).wait_send())
        if k < 4:

            @pl.when(c != k % 2)
            def _(k=k):
                owner_copy(k, 0).wait_send()

    def arrival(group, d):
        return remote(
            turned.at[0, 0], operator.at[0, group], o_send.at[0, 0], o_recv.at[group, d], sibling
        )

    for group in range(5):
        each_other(lambda d, group=group: arrival(group, d).wait_recv())
        if group < 4:

            @pl.when(c != group // 2)
            def _(group=group):
                arrival(group, 0).wait_recv()

    matrix = operator[...].reshape(640, 640)
    term = wv[0]
    total = term
    for degree in range(1, 5):
        term = jnp.dot(matrix, term.astype(BF16), preferred_element_type=F32) * (1.0 / degree)
        total = total + term
    out[0] = total


def hand_over(walkers_in, aux_in, walkers_out, aux_out, walkers, aux, sem):
    ins = [
        pltpu.make_async_copy(walkers_in, walkers, sem.at[0]),
        pltpu.make_async_copy(aux_in, aux, sem.at[1]),
    ]
    outs = [
        pltpu.make_async_copy(walkers, walkers_out, sem.at[2]),
        pltpu.make_async_copy(aux, aux_out, sem.at[3]),
    ]
    for copy in ins:
        copy.start()
    for copy, following in zip(ins, outs):
        copy.wait()
        following.start()
    for copy in outs:
        copy.wait()


def shape(*dims, dtype=BF16):
    return jax.ShapeDtypeStruct(dims, dtype)


def room(*dims, dtype=BF16):
    return pltpu.VMEM(dims, dtype)


def dma(*dims):
    return pltpu.SemaphoreType.DMA(dims)


def body(walkers, intersection_inverse, aux_draws, chol_half, chol_full):
    new_walkers, aux = pl.pallas_call(
        kernel,
        out_shape=(shape(1, 640, 128, dtype=F32), shape(192, 256, dtype=F32)),
        in_specs=[ANY] * 5,
        out_specs=(VMEM, VMEM),
        scratch_shapes=[
            room(1, 640, 128, dtype=F32),
            room(1, 128, 128, dtype=F32),
            room(192, 256, dtype=F32),
            room(192, 40, 128),
            room(192, 40, 640),
            room(16, 40, 128),
            room(16, 40, 128),
            room(16, 40, 16, 128),
            room(40, 192, 128),
            room(3, 8, 2, 192, 640),
            room(2, 8, 192, 640),
            room(16, 16, 192),
            room(16, 16, 192),
            room(16, 16, 192),
            room(2, 2, 8, 16, 192),
            room(5, 4, 2, 8, 16, 640),
            room(4, 2, 4, 16, 640),
            room(4, 2, 4, 16, 640),
            room(4, 2, 8, 16, 640),
            room(4, 2, 8, 16, 640),
            room(4, 8, 16, 640),
            room(4, 8, 16, 640),
            room(4, 8, 16, 640),
            room(4, 8, 16, 640),
            room(4, 16, 640),
            room(4, 16, 640),
            room(8, 16, 640),
            room(8, 16, 640),
            room(5, 16, 8, 640),
            room(16, 5, 8, 640),
            dma(5), dma(3), dma(3), dma(16), dma(16), dma(17), dma(17), dma(16), dma(16), dma(16), dma(16),
            dma(), dma(), dma(5, 3), dma(5, 3), dma(5, 3), dma(5, 3), dma(5), dma(5), dma(5, 16), dma(5, 16),
        ],
        compiler_params=pltpu.CompilerParams(
            collective_id=0, has_side_effects=True, vmem_limit_bytes=60 * 2**20
        ),
        name="propagate",
    )(walkers, intersection_inverse, aux_draws.T, chol_half, chol_full)
    new_walkers, aux = pl.pallas_call(
        hand_over,
        out_shape=(shape(1, 640, 128, dtype=F32), shape(192, 256, dtype=F32)),
        in_specs=[ANY] * 2,
        out_specs=(ANY, ANY),
        scratch_shapes=[room(1, 640, 128, dtype=F32), room(192, 256, dtype=F32), dma(4)],
        name="hand_over",
    )(new_walkers, aux)
    return new_walkers, aux.T


def solution(mesh):
    placed = (
        P(("walk", "chol"), None, None),
        P(("walk", "chol"), None, None),
        P(None, "chol"),
        P("chol", "walk", None),
        P("chol", "walk", None),
    )
    return jax.shard_map(
        body,
        mesh=mesh,
        in_specs=placed,
        out_specs=(P(("walk", "chol"), None, None), P(None, "chol")),
        check_vma=False,
    )
```

time: 334 us -> 124 us (0.37)
  waiting for transfers between devices: 202 us -> 0 us
  Pallas kernels: 0 us -> 122 us
  blocking collectives: 65.2 us -> 0 us
  starting transfers between devices: 17.3 us -> 0 us
  matrix products: 16.9 us -> 0 us
  local copies, waits for them, and re-layouts: 16.8 us -> 0 us
  between operations: 14.2 us -> 0.64 us
    reduce_scatter x1 -> x0, waiting for transfers between devices: 140 us -> none  [body(): lax.psum_scatter(jnp.dot(field_low, full_flat, preferred_element_type=jnp...]
    pallas_call x0 -> x2, Pallas kernels: none -> 122 us  [the longest x1 120 us: body(): pl.pallas_call(kernel, out_shape=(shape(1, 640, 128, dtype=F32), shape(19...]
    all_gather x1 -> x0, blocking collectives: 43.1 us -> none  [body(): lax.all_gather(own_bias, 'walk', axis=0, tiled=True).astype(jnp.float32)]
    all_gather x1 -> x0, waiting for transfers between devices: 36.7 us -> none  [body(): piece = lax.all_gather(green_slab, 'chol', axis=0, tiled=True)]
    all_to_all x2 -> x0, waiting for transfers between devices: 25.3 us -> none  [the longest x1 23.6 us: body(): lax.all_to_all(operator, 'walk', split_axis=0, concat_axis=1, tiled=True)]
    all_to_all x1 -> x0, blocking collectives: 22.1 us -> none  [body(): lax.all_to_all(green_half, 'walk', split_axis=1, concat_axis=0, tiled=True)]
    all_to_all x2 -> x0, starting transfers between devices: 17.2 us -> none  [the longest x1 8.63 us: body(): lax.all_to_all(operator, 'walk', split_axis=0, concat_axis=1, tiled=True)]
    dot_general x7 -> x0, matrix products: 16.9 us -> none  [the longest x1 10.3 us: body(): jnp.dot(field_low, full_flat, preferred_element_type=jnp.float32)]
  transfers between devices with their start and end apart: 4 -> 0, of which waited for: 4 -> 0; matrix products, arithmetic and copies ran while one was open for 4% -> 0% of each run, Pallas kernels for 0% -> 0%
where the time goes in v3:
time: 124 us; the launch traced here: 123 us
  Pallas kernels  122 us (98%)
    pallas_call x1, Pallas kernels, body(): pl.pallas_call(kernel, out_shape=(shape(1, 640, 128, dtype=F32), shape(19...  120 us

profile of v3, /device:TPU:8, one launch (start us, length us, event | category | flops | bytes accessed | tf_op | source)
XLA Modules:
  0.0 122.7 jit_solution(4922801320068693107)
XLA Ops:
  0.6 120.2 %propagate.1 = (f32[1,640,128]{2,1,0:T(8,128)}, f32[192,256]{1,0:T(8,128)}) custom-call(f32[1,640,128]{2,1,0:T(8,128)} %walkers.1, f32[1,128,128]{2,1,0:T(8,128)} %inverse.1, f32[192,256]{1,0:T(8,128)} %bitcast.2, bf16[192,40,128]{2,1,0:T(8,128)(2,1)} %half.1, bf16[192,40,640]{2,1,0:T(8,128)(2,1)} %full.1), custom_call_target="tpu_custom_call" | custom-call | tf_op jit(solution)/shard_map/propagate/pallas_call | solution.py:464
  120.9 1.8 %hand_over.1 = (f32[1,640,128]{2,1,0:T(8,128)}, f32[192,256]{1,0:T(8,128)}) custom-call(f32[1,640,128]{2,1,0:T(8,128)} %get-tuple-element.6.walkers_in, f32[192,256]{1,0:T(8,128)} %get-tuple-element.7.aux_in), custom_call_target="tpu_custom_call" | custom-call | tf_op jit(solution)/shard_map/hand_over/pallas_call | solution.py:508

commit v4 on v3

v4 whole, which is shorter than its diff:
```python
import jax
import jax.numpy as jnp
from jax import lax
from jax.experimental import pallas as pl
from jax.experimental.pallas import tpu as pltpu
from jax.sharding import PartitionSpec as P

MESH = pl.DeviceIdType.MESH
BF16 = jnp.bfloat16
F32 = jnp.float32
ANY = pl.BlockSpec(memory_space=pl.ANY)
VMEM = pl.BlockSpec(memory_space=pltpu.VMEM)


def place():
    a = lax.axis_index("walk")
    b = lax.axis_index("chol")
    return a, b // 4, (b // 2) % 2, b % 2


def at(a, y, z, c):
    return (a, y * 4 + z * 2 + c)


def remote(src, dst, send, recv, target):
    return pltpu.make_async_remote_copy(
        src_ref=src, dst_ref=dst, send_sem=send, recv_sem=recv, device_id=target, device_id_type=MESH
    )


def settle(ref, sem):
    a, y, z, c = place()
    remote(ref, ref, sem, sem, at(a, y, z, 1 - c)).wait_recv()


def greet(target):
    pl.semaphore_signal(pltpu.get_barrier_semaphore(), inc=1, device_id=target, device_id_type=MESH)


def kernel(
    walkers, inverse, draws, half, full,
    out, aux_out,
    wv, iv, dv, hv, fv, gsend, blocks, gt, ht, ct, given, dj, pb, xin, zhin, ball, field,
    part, pass_up, pass_down, from_down, from_up, z_out, from_z,
    zin, zsum, z_pass_up, z_pass_down, z_from_down, z_from_up, turned, operator, term1,
    in_sem, ct_send, ct_recv, a_send, a_recv, g_send, g_recv, p_send, p_recv, q_send, q_recv,
    b_send, b_recv, f_send, f_recv, y_send, far_in, near_in, last_in, z_send, z_in, o_send, o_recv,
):
    a, y, z, c = place()
    x, zh = a // 4, a % 4
    up, down, far = (y + 1) % 4, (y + 3) % 4, (y + 2) % 4
    to_up, to_down, to_z = at(a, up, z, c), at(a, down, z, c), at(a, y, 1 - z, c)
    sibling = at(a, y, z, 1 - c)

    def load(index):
        pair = ((walkers, wv), (inverse, iv), (half, hv), (full, fv), (draws, dv))[index]
        return pltpu.make_async_copy(pair[0], pair[1], in_sem.at[index])

    for index in range(5):
        load(index).start()

    def greet_walk(d, _):
        greet(at((a + d) % 16, y, z, c))
        greet(at((a + d) % 16, y, z, 1 - c))
        return 0

    lax.fori_loop(1, 16, greet_walk, 0)
    round_chol = (
        at(a, far, 1 - z, c), at(a, far, z, c), at(a, up, 1 - z, c), at(a, down, 1 - z, c),
        to_up, to_down, to_z, sibling,
    )
    for target in round_chol:
        greet(target)

    load(0).wait()
    load(1).wait()
    green = jnp.dot(
        wv[0], iv[0], precision=lax.Precision.HIGHEST, preferred_element_type=F32
    ).astype(BF16)
    gsend[...] = green.reshape(16, 40, 128)
    pl.semaphore_wait(pltpu.get_barrier_semaphore(), 38)

    def each_other(step):
        def run(d, _):
            step(d)
            return 0

        lax.fori_loop(1, 16, run, 0)

    def peer(d):
        return (a + d) % 16

    def slot(yy, zz):
        return c * 8 + yy * 2 + zz

    own = slot(y, z)

    def green_copy(to):
        return remote(
            gsend.at[to], blocks.at[own, a % 2, a // 2], a_send, a_recv.at[a % 2], at(to, y, z, c)
        )

    each_other(lambda d: green_copy(peer(d)).start())
    blocks[own, a % 2, a // 2] = gsend[a]

    load(2).wait()

    def turn_half(i, _):
        n0 = pl.multiple_of(i * 16, 16)
        ht[:, pl.ds(n0, 16), :] = jnp.swapaxes(hv[pl.ds(n0, 16)], 0, 1)
        return 0

    lax.fori_loop(0, 12, turn_half, 0)

    load(3).wait()

    def turn_full(group, target):
        def turn(i, _):
            n0 = pl.multiple_of(i * 16, 16)
            target[:, pl.ds(n0, 16), :] = jnp.swapaxes(
                fv[pl.ds(n0, 16), group * 8 : group * 8 + 8, :], 0, 1
            )
            return 0

        lax.fori_loop(0, 12, turn, 0)

    def turn_given(i):
        for core in range(2):

            @pl.when(c == core)
            def _(core=core):
                turn_full(2 * (1 - core) + i, given.at[i])

    def turn_kept(i):
        for core in range(2):

            @pl.when(c == core)
            def _(core=core):
                turn_full(2 * core + i, ct.at[i, :, core])

    def give(i):
        source = ct.at[2, :, c] if i == 2 else given.at[i]
        return remote(source, ct.at[i, :, c], ct_send, ct_recv, sibling)

    turn_given(0)
    give(0).start()

    def wait_green(h):
        @pl.when(a % 2 == h)
        def _():
            settle(blocks.at[0, h, pl.ds(0, 7)], a_recv.at[h])

        @pl.when(a % 2 != h)
        def _():
            settle(blocks.at[0, h], a_recv.at[h])

    origins = (
        (far, 1 - z), (far, z), (down, 1 - z), (up, 1 - z), (down, z), (up, z), (y, 1 - z),
    )

    def spread(h, index):
        yy, zz = (y, z) if index < 8 else origins[index - 8]
        target = round_chol[index] if index < 8 else sibling
        ref = blocks.at[slot(yy, zz), h]
        return remote(ref, ref, g_send, g_recv.at[h, min(index, 7)], target)

    def spread_own(h):
        for index in range(8):
            spread(h, index).start()

    def spread_on(h):
        for index in (6, 5, 4, 3, 2, 1, 0):
            settle(blocks.at[0, h], g_recv.at[h, index])
            spread(h, 8 + index).start()
        settle(blocks.at[pl.ds(0, 4)], g_recv.at[h, 7])

    def bias_sums(h):
        def turn(i, _):
            both = blocks[pl.ds(2 * i, 2), h].reshape(16, 40, 128)
            gt[h, :, i] = jnp.swapaxes(both, 0, 1)
            return 0

        lax.fori_loop(0, 8, turn, 0)

        def step(i, acc):
            p0 = i * 8
            left = jnp.concatenate([gt[h, p0 + q].reshape(128, 128) for q in range(8)], axis=1)
            right = jnp.concatenate([ht[p0 + q] for q in range(8)], axis=1)
            return acc + lax.dot_general(
                left, right, (((1,), (1,)), ((), ())), preferred_element_type=F32
            )

        partial = lax.fori_loop(0, 5, step, jnp.zeros((128, 192), F32))
        pb[4 * h : 4 * h + 4] = partial.astype(BF16).reshape(4, 32, 192)

    def x_peer(e):
        return (x + e) % 4

    def x_copy(h, e):
        return remote(
            pb.at[4 * h + x_peer(e)], xin.at[h, x], p_send, p_recv.at[h],
            at(x_peer(e) * 4 + zh, y, z, c),
        )

    def zh_copy(h, e):
        ref = zhin.at[h, zh]
        return remote(ref, ref, q_send, q_recv.at[h], at(x * 4 + (zh + e) % 4, y, z, c))

    def back_copy(h, e):
        ref = ball.at[h, x]
        return remote(ref, ref, b_send, b_recv.at[h], at(x_peer(e) * 4 + zh, y, z, c))

    def start_x(h):
        for e in (2, 1, 3):
            x_copy(h, e).start()
        xin[h, x] = pb[4 * h + x]

    def start_zh(h):
        settle(xin.at[h, pl.ds(0, 3)], p_recv.at[h])
        zhin[h, zh] = jnp.sum(xin[h].astype(F32), axis=0).astype(BF16)
        for e in (2, 1, 3):
            zh_copy(h, e).start()

    def start_back(h):
        settle(zhin.at[h, pl.ds(0, 3)], q_recv.at[h])
        ball[h, x] = jnp.sum(zhin[h].astype(F32), axis=0).astype(BF16)
        for e in (2, 1, 3):
            back_copy(h, e).start()

    def field_copy(h):
        ref = field.at[c, h]
        return remote(ref, ref, f_send, f_recv.at[h], sibling)

    def field_arrived(h):
        settle(field.at[0, h], f_recv.at[h])

    def shift(h):
        settle(ball.at[h, pl.ds(0, 3)], b_recv.at[h])
        shifted = dj[h] - ball[h].astype(F32).reshape(2, 8, 8, 192)
        dj[h] = shifted
        field[c, h] = shifted.astype(BF16).reshape(2, 64, 192)
        field_copy(h).start()

    wait_green(0)
    spread_own(0)
    wait_green(1)
    spread_own(1)
    turn_given(1)
    give(1).start()
    for core in range(2):

        @pl.when(c == core)
        def _(core=core):
            turn_full(4, ct.at[2, :, core])

    give(2).start()
    turn_kept(0)
    turn_kept(1)
    load(4).wait()
    by_walker = dv[...].T.reshape(8, 2, 16, 192)
    for h in range(2):
        half_draws = jnp.swapaxes(by_walker[:, h], 0, 1).reshape(8, 2, 8, 192)
        for core in range(2):
            dj[h, core] = half_draws[:, core]
    spread_on(0)
    bias_sums(0)
    start_x(0)
    start_zh(0)
    spread_on(1)
    bias_sums(1)
    start_x(1)
    start_back(0)
    start_zh(1)
    shift(0)
    settle(ct.at[:, :, 1 - c], ct_recv)
    field_arrived(0)

    low, high = pl.ds(0, 4), pl.ds(4, 4)

    def multiply(pair, first_row, last_row):
        left = [field[s, pair // 2].reshape(128, 192) for s in range(2)]

        def row(r, _):
            value = jnp.dot(left[0], ct[pair % 2, r, 0], preferred_element_type=F32)
            value = value + jnp.dot(left[1], ct[pair % 2, r, 1], preferred_element_type=F32)
            value = value.astype(BF16).reshape(2, 4, 2, 8, 640)
            for core in range(2):
                part[2 * pair + core, :, :, r] = value[core]
            return 0

        lax.fori_loop(first_row, last_row, row, 0)

    def multiply_z(h):
        left = [field[s, h, c] for s in range(2)]

        def row(r, _):
            value = jnp.dot(left[0], ct[2, r, 0], preferred_element_type=F32)
            value = value + jnp.dot(left[1], ct[2, r, 1], preferred_element_type=F32)
            part[8 + h, :, :, r] = value.astype(BF16).reshape(4, 2, 8, 640)
            return 0

        lax.fori_loop(0, 8, row, 0)
        z_copy(8 + h).start()

    def z_copy(k):
        if k >= 8:
            return remote(part.at[k, :, 1 - z], zin.at[k - 8], z_send, z_in.at[k - 8], to_z)
        return remote(z_out.at[k], from_z.at[k], z_send, last_in.at[k], to_z)

    def sum_z(k):
        settle(zin.at[k - 8], z_in.at[k - 8])
        total = part[k, :, z].astype(F32) + zin[k - 8].astype(F32)
        zsum[k - 8] = total.astype(BF16)

    def arrivals(k, step):
        return (far_in, near_in, near_in, last_in)[step].at[k]

    def send_up(k, step):
        if k >= 8:
            pair = (
                (zsum.at[k - 8, far, low], z_pass_up.at[k - 8]),
                (zsum.at[k - 8, up, high], z_from_down.at[k - 8, high]),
                (z_pass_up.at[k - 8], z_from_down.at[k - 8, low]),
            )[step]
        else:
            pair = (
                (part.at[k, far, :, low], pass_up.at[k]),
                (part.at[k, up, :, high], from_down.at[k, :, high]),
                (pass_up.at[k, 1 - z], from_down.at[k, 1 - z, low]),
                (pass_up.at[k, z], from_down.at[k, z, low]),
            )[step]
        return remote(pair[0], pair[1], y_send.at[k // 8], arrivals(k, step), to_up)

    def send_down(k, step):
        if k >= 8:
            pair = (
                (zsum.at[k - 8, far, high], z_pass_down.at[k - 8]),
                (zsum.at[k - 8, down, low], z_from_up.at[k - 8, low]),
                (z_pass_down.at[k - 8], z_from_up.at[k - 8, high]),
            )[step]
        else:
            pair = (
                (part.at[k, far, :, high], pass_down.at[k]),
                (part.at[k, down, :, low], from_up.at[k, :, low]),
                (pass_down.at[k, 1 - z], from_up.at[k, 1 - z, high]),
                (pass_down.at[k, z], from_up.at[k, z, high]),
            )[step]
        return remote(pair[0], pair[1], y_send.at[k // 8], arrivals(k, step), to_down)

    def begin(k, *which):
        for step in which or (0, 1):
            send_up(k, step).start()
            send_down(k, step).start()

    def pass_on(k):
        settle(z_from_down.at[k - 8] if k >= 8 else from_down.at[k], far_in.at[k])
        if k >= 8:
            total = z_pass_up[k - 8].astype(F32) + zsum[k - 8, up, 0:4].astype(F32)
            z_pass_up[k - 8] = total.astype(BF16)
            send_up(k, 2).start()
            total = z_pass_down[k - 8].astype(F32) + zsum[k - 8, down, 4:8].astype(F32)
            z_pass_down[k - 8] = total.astype(BF16)
            send_down(k, 2).start()
            return
        for zz, step in ((1 - z, 2), (z, 3)):
            total = pass_up[k, zz].astype(F32) + part[k, up, zz, 0:4].astype(F32)
            pass_up[k, zz] = total.astype(BF16)
            send_up(k, step).start()
            total = pass_down[k, zz].astype(F32) + part[k, down, zz, 4:8].astype(F32)
            pass_down[k, zz] = total.astype(BF16)
            send_down(k, step).start()

    def gathered(k):
        settle(from_down.at[0] if k >= 8 else pass_up.at[pl.ds(0, 3)], near_in.at[k])

    def over_z(k):
        gathered(k)
        other = 1 - z
        total = part[k, y, other].astype(F32) + from_down[k, other].astype(F32)
        z_out[k] = (total + from_up[k, other].astype(F32)).astype(BF16)
        z_copy(k).start()

    def group_of(k):
        return 4 if k >= 8 else 2 * c + (k // 2) % 2

    def core_of(k):
        return c if k >= 8 else k % 2

    def half_of(k):
        return k - 8 if k >= 8 else k // 4

    def walk_of(k, i):
        return 2 * i + half_of(k)

    def owner_copy(k, i):
        group = group_of(k)
        return remote(
            turned.at[8 * k + i], operator.at[group, a], o_send, o_recv.at[group],
            at(walk_of(k, i), y, z, core_of(k)),
        )

    def each_owner(k, other, own=None):
        def run(d, _):
            i = (a + d) % 8
            here = jnp.logical_and(walk_of(k, i) == a, core_of(k) == c)

            @pl.when(jnp.logical_not(here))
            def _():
                other(i)

            if own is not None:

                @pl.when(here)
                def _():
                    own(i)

            return 0

        lax.fori_loop(0, 8, run, 0)

    def deliver(k):
        if k >= 8:
            gathered(k)
            total = zsum[k - 8, y].astype(F32) + z_from_down[k - 8].astype(F32)
            total = total + z_from_up[k - 8].astype(F32)
        else:
            settle(from_down.at[k], last_in.at[k])
            total = part[k, y, z].astype(F32) + from_down[k, z].astype(F32)
            total = total + from_up[k, z].astype(F32) + from_z[k].astype(F32)
        turned[8 * k : 8 * k + 8] = jnp.swapaxes(total, 0, 1).astype(BF16)

        def keep(i):
            operator[group_of(k), a] = turned[8 * k + i]

        each_owner(k, lambda i: owner_copy(k, i).start(), keep)

    multiply(0, 0, 4)
    send_up(0, 0).start()
    send_down(0, 1).start()
    multiply(0, 4, 8)
    send_down(0, 0).start()
    send_up(0, 1).start()
    begin(1)
    multiply_z(0)
    multiply(1, 0, 8)
    start_back(1)
    pass_on(0)
    begin(2)
    pass_on(1)
    begin(3)
    shift(1)
    field_arrived(1)
    multiply_z(1)
    multiply(2, 0, 8)
    over_z(0)
    pass_on(2)
    begin(4)
    multiply(3, 0, 8)
    over_z(1)
    pass_on(3)
    begin(5)
    sum_z(8)
    begin(8)
    by_half = [
        jnp.swapaxes(jnp.swapaxes(dj[h], 0, 1).reshape(16, 8, 192), 0, 1) for h in range(2)
    ]
    aux_out[...] = jnp.stack(by_half, axis=1).reshape(256, 192).T
    over_z(2)
    pass_on(4)
    begin(6)
    deliver(0)
    deliver(1)
    over_z(3)
    pass_on(5)
    deliver(2)
    pass_on(8)
    begin(7)
    deliver(3)
    over_z(4)
    pass_on(6)
    sum_z(9)
    begin(9, 0)
    deliver(4)
    over_z(5)
    deliver(8)
    pass_on(7)
    begin(9, 1)
    deliver(5)
    over_z(6)
    pass_on(9)
    over_z(7)
    deliver(6)
    deliver(9)
    deliver(7)

    settle(gsend.at[pl.ds(0, 15)], a_send)
    settle(ct.at[:, :, c], ct_send)
    settle(blocks.at[pl.ds(0, 15)], g_send)
    settle(pb.at[pl.ds(0, 6)], p_send)
    settle(pb.at[pl.ds(0, 6)], q_send)
    settle(pb.at[pl.ds(0, 6)], b_send)
    settle(field.at[0], f_send)
    settle(part.at[pl.ds(0, 6)], y_send.at[0])
    settle(pass_up.at[pl.ds(0, 6)], y_send.at[1])
    settle(from_down, z_send)

    def wait_group(group):
        core = c if group == 4 else group // 2

        @pl.when(core == c)
        def _():
            settle(operator.at[group, pl.ds(0, 15)], o_recv.at[group])

        @pl.when(core != c)
        def _():
            settle(operator.at[group], o_recv.at[group])

    start_low = wv[0].astype(BF16)
    for group in (0, 2, 1, 3, 4):
        wait_group(group)
        rows = operator[group].reshape(128, 640)
        value = jnp.dot(rows, start_low, preferred_element_type=F32)
        term1[:, group] = value.reshape(16, 8, 128)
    settle(turned.at[pl.ds(0, 77)], o_send)
    matrix = jnp.swapaxes(operator[...], 0, 1).reshape(640, 640)
    term = term1[...].reshape(640, 128)
    total = wv[0] + term
    for degree in range(2, 5):
        term = jnp.dot(matrix, term.astype(BF16), preferred_element_type=F32) * (1.0 / degree)
        total = total + term
    out[0] = total


def hand_over(walkers_in, aux_in, walkers_out, aux_out, walkers, aux, sem):
    ins = [
        pltpu.make_async_copy(walkers_in, walkers, sem.at[0]),
        pltpu.make_async_copy(aux_in, aux, sem.at[1]),
    ]
    outs = [
        pltpu.make_async_copy(walkers, walkers_out, sem.at[2]),
        pltpu.make_async_copy(aux, aux_out, sem.at[3]),
    ]
    for copy in ins:
        copy.start()
    for copy, following in zip(ins, outs):
        copy.wait()
        following.start()
    for copy in outs:
        copy.wait()


def shape(*dims, dtype=BF16):
    return jax.ShapeDtypeStruct(dims, dtype)


def room(*dims, dtype=BF16):
    return pltpu.VMEM(dims, dtype)


def dma(*dims):
    return pltpu.SemaphoreType.DMA(dims)


def body(walkers, intersection_inverse, aux_draws, chol_half, chol_full):
    new_walkers, aux = pl.pallas_call(
        kernel,
        out_shape=(shape(1, 640, 128, dtype=F32), shape(192, 256, dtype=F32)),
        in_specs=[ANY] * 5,
        out_specs=(VMEM, VMEM),
        scratch_shapes=[
            room(1, 640, 128, dtype=F32),
            room(1, 128, 128, dtype=F32),
            room(192, 256, dtype=F32),
            room(192, 40, 128),
            room(192, 40, 640),
            room(16, 40, 128),
            room(16, 2, 8, 40, 128),
            room(2, 40, 8, 16, 128),
            room(40, 192, 128),
            room(3, 8, 2, 192, 640),
            room(2, 8, 192, 640),
            room(2, 2, 8, 8, 192, dtype=F32),
            room(8, 32, 192),
            room(2, 4, 32, 192),
            room(2, 4, 32, 192),
            room(2, 4, 32, 192),
            room(2, 2, 2, 64, 192),
            room(10, 4, 2, 8, 8, 640),
            room(8, 2, 4, 8, 640),
            room(8, 2, 4, 8, 640),
            room(8, 2, 8, 8, 640),
            room(8, 2, 8, 8, 640),
            room(8, 8, 8, 640),
            room(8, 8, 8, 640),
            room(2, 4, 8, 8, 640),
            room(2, 4, 8, 8, 640),
            room(2, 4, 8, 640),
            room(2, 4, 8, 640),
            room(2, 8, 8, 640),
            room(2, 8, 8, 640),
            room(80, 8, 640),
            room(5, 16, 8, 640),
            room(16, 5, 8, 128, dtype=F32),
            dma(5), dma(), dma(), dma(), dma(2), dma(), dma(2, 8), dma(), dma(2), dma(), dma(2),
            dma(), dma(2), dma(), dma(2), dma(2), dma(10), dma(10), dma(8), dma(), dma(2), dma(), dma(5),
        ],
        compiler_params=pltpu.CompilerParams(
            collective_id=0, has_side_effects=True, vmem_limit_bytes=60 * 2**20
        ),
        name="propagate",
    )(walkers, intersection_inverse, aux_draws.T, chol_half, chol_full)
    new_walkers, aux = pl.pallas_call(
        hand_over,
        out_shape=(shape(1, 640, 128, dtype=F32), shape(192, 256, dtype=F32)),
        in_specs=[ANY] * 2,
        out_specs=(ANY, ANY),
        scratch_shapes=[room(1, 640, 128, dtype=F32), room(192, 256, dtype=F32), dma(4)],
        name="hand_over",
    )(new_walkers, aux)
    return new_walkers, aux.T


def solution(mesh):
    placed = (
        P(("walk", "chol"), None, None),
        P(("walk", "chol"), None, None),
        P(None, "chol"),
        P("chol", "walk", None),
        P("chol", "walk", None),
    )
    return jax.shard_map(
        body,
        mesh=mesh,
        in_specs=placed,
        out_specs=(P(("walk", "chol"), None, None), P(None, "chol")),
        check_vma=False,
    )
```

time: 124 us -> 112 us (0.903)
  the two profiles are of different devices: /device:TPU:8 before, /device:TPU:65 now
where the time goes in v4:
time: 112 us
  Pallas kernels  111 us (99%)
    pallas_call x1, Pallas kernels, body(): pl.pallas_call(kernel, out_shape=(shape(1, 640, 128, dtype=F32), shape(19...  110 us

profile of v4, /device:TPU:65, one launch (start us, length us, event | category | flops | bytes accessed | tf_op | source)
XLA Modules:
  0.0 112.0 jit_solution(1248413887783067401)
XLA Ops:
  0.6 109.6 %propagate.1 = (f32[1,640,128]{2,1,0:T(8,128)}, f32[192,256]{1,0:T(8,128)}) custom-call(f32[1,640,128]{2,1,0:T(8,128)} %walkers.1, f32[1,128,128]{2,1,0:T(8,128)} %inverse.1, f32[192,256]{1,0:T(8,128)} %bitcast.2, bf16[192,40,128]{2,1,0:T(8,128)(2,1)} %half.1, bf16[192,40,640]{2,1,0:T(8,128)(2,1)} %full.1), custom_call_target="tpu_custom_call" | custom-call | tf_op jit(solution)/shard_map/propagate/pallas_call | solution.py:565
  110.2 1.8 %hand_over.1 = (f32[1,640,128]{2,1,0:T(8,128)}, f32[192,256]{1,0:T(8,128)}) custom-call(f32[1,640,128]{2,1,0:T(8,128)} %get-tuple-element.6.walkers_in, f32[192,256]{1,0:T(8,128)} %get-tuple-element.7.aux_in), custom_call_target="tpu_custom_call" | custom-call | tf_op jit(solution)/shard_map/hand_over/pallas_call | solution.py:612

commit v5 on v4

--- a/solution.py
+++ b/solution.py
@@ -40,7 +40,7 @@
 def kernel(
     walkers, inverse, draws, half, full,
     out, aux_out,
-    wv, iv, dv, hv, fv, gsend, blocks, gt, ht, ct, given, dj, pb, xin, zhin, ball, field,
+    wv, iv, dv, hv, fv, gsend, blocks, gt, ht, ct, given, order, dj, pb, xin, zhin, ball, field,
     part, pass_up, pass_down, from_down, from_up, z_out, from_z,
     zin, zsum, z_pass_up, z_pass_down, z_from_down, z_from_up, turned, operator, term1,
     in_sem, ct_send, ct_recv, a_send, a_recv, g_send, g_recv, p_send, p_recv, q_send, q_recv,
@@ -61,15 +61,25 @@
 
     def greet_walk(d, _):
         greet(at((a + d) % 16, y, z, c))
-        greet(at((a + d) % 16, y, z, 1 - c))
         return 0
 
     lax.fori_loop(1, 16, greet_walk, 0)
-    round_chol = (
-        at(a, far, 1 - z, c), at(a, far, z, c), at(a, up, 1 - z, c), at(a, down, 1 - z, c),
-        to_up, to_down, to_z, sibling,
-    )
-    for target in round_chol:
+
+    def greet_senders(d, _):
+        xx, core = d // 2, d % 2
+
+        @pl.when(jnp.logical_or(xx != x, core != c))
+        def _():
+            greet(at(xx * 4 + zh, y, z, core))
+
+        greet(at(xx * 4 + (zh + 2) % 4, y, 1 - z, core))
+        greet(at(xx * 4 + (zh + 3) % 4, y, 1, core))
+        greet(at(xx * 4 + (zh + 1) % 4, y, 0, core))
+        return 0
+
+    lax.fori_loop(0, 8, greet_senders, 0)
+    to_far = at(a, far, z, c)
+    for target in (to_far, to_up, to_down, to_z, sibling):
         greet(target)
 
     load(0).wait()
@@ -78,7 +88,7 @@
         wv[0], iv[0], precision=lax.Precision.HIGHEST, preferred_element_type=F32
     ).astype(BF16)
     gsend[...] = green.reshape(16, 40, 128)
-    pl.semaphore_wait(pltpu.get_barrier_semaphore(), 38)
+    pl.semaphore_wait(pltpu.get_barrier_semaphore(), 51)
 
     def each_other(step):
         def run(d, _):
@@ -100,7 +110,10 @@
             gsend.at[to], blocks.at[own, a % 2, a // 2], a_send, a_recv.at[a % 2], at(to, y, z, c)
         )
 
-    each_other(lambda d: green_copy(peer(d)).start())
+    @pl.when(a % 2 == 0)
+    def _():
+        each_other(lambda d: green_copy(peer(d)).start())
+
     blocks[own, a % 2, a // 2] = gsend[a]
 
     load(2).wait()
@@ -144,6 +157,42 @@
 
     turn_given(0)
     give(0).start()
+    turn_given(1)
+    give(1).start()
+    for core in range(2):
+
+        @pl.when(c == core)
+        def _(core=core):
+            turn_full(4, ct.at[2, :, core])
+
+    give(2).start()
+
+    @pl.when(a % 2 == 1)
+    def _():
+        each_other(lambda d: green_copy(peer(d)).start())
+
+    turn_kept(0)
+    turn_kept(1)
+
+    def owner(h, zl, i):
+        same = 1 - (zh + h) % 2
+        pick = i % 2
+        to_zh = (zh + same * 2 * pick + (1 - same) * (3 - 2 * zl)) % 4
+        return i // 2, to_zh, same * ((zl + pick) % 2) + (1 - same) * pick
+
+    for h in range(2):
+        row = lax.broadcasted_iota(jnp.int32, (64, 64), 0)
+        column = lax.broadcasted_iota(jnp.int32, (64, 64), 1)
+        to_x, to_zh, to_zl = owner(h, (row // 8) % 2, row % 8)
+        source = (row // 16) * 16 + to_zl * 8 + to_x * 2 + to_zh // 2
+        order[h] = jnp.where(source == column, 1.0, 0.0).astype(BF16)
+
+    load(4).wait()
+    by_walker = dv[...].T.reshape(8, 2, 16, 192)
+    for h in range(2):
+        half_draws = jnp.swapaxes(by_walker[:, h], 0, 1).reshape(8, 2, 8, 192)
+        for core in range(2):
+            dj[h, core] = half_draws[:, core]
 
     def wait_green(h):
         @pl.when(a % 2 == h)
@@ -154,25 +203,37 @@
         def _():
             settle(blocks.at[0, h], a_recv.at[h])
 
-    origins = (
-        (far, 1 - z), (far, z), (down, 1 - z), (up, 1 - z), (down, z), (up, z), (y, 1 - z),
-    )
-
     def spread(h, index):
-        yy, zz = (y, z) if index < 8 else origins[index - 8]
-        target = round_chol[index] if index < 8 else sibling
+        yy, zz, target = (
+            (y, z, to_far), (y, z, to_up), (y, z, to_down), (y, z, to_z), (y, z, sibling),
+            (y, 1 - z, to_up), (y, 1 - z, to_down), (far, z, to_z),
+            (y, 1 - z, sibling), (far, z, sibling), (down, z, sibling), (up, z, sibling),
+            (down, 1 - z, sibling), (up, 1 - z, sibling), (far, 1 - z, sibling),
+        )[index]
         ref = blocks.at[slot(yy, zz), h]
-        return remote(ref, ref, g_send, g_recv.at[h, min(index, 7)], target)
+        return remote(ref, ref, g_send, g_recv.at[h, index if index < 8 else 4], target)
+
+    def start(h, *indices):
+        for index in indices:
+            spread(h, index).start()
+
+    def landed(h, index):
+        settle(blocks.at[0, h], g_recv.at[h, index])
 
     def spread_own(h):
-        for index in range(8):
-            spread(h, index).start()
+        start(h, 3, 0, 1, 2, 4)
+
+    def spread_second(h):
+        landed(h, 3)
+        start(h, 5, 6, 8)
+        landed(h, 0)
+        start(h, 7, 9)
 
     def spread_on(h):
-        for index in (6, 5, 4, 3, 2, 1, 0):
-            settle(blocks.at[0, h], g_recv.at[h, index])
-            spread(h, 8 + index).start()
-        settle(blocks.at[pl.ds(0, 4)], g_recv.at[h, 7])
+        for index in (1, 2, 5, 6, 7):
+            landed(h, index)
+            start(h, {1: 10, 2: 11, 5: 12, 6: 13, 7: 14}[index])
+        settle(blocks.at[pl.ds(0, 4)], g_recv.at[h, 4])
 
     def bias_sums(h):
         def turn(i, _):
@@ -238,39 +299,26 @@
         settle(ball.at[h, pl.ds(0, 3)], b_recv.at[h])
         shifted = dj[h] - ball[h].astype(F32).reshape(2, 8, 8, 192)
         dj[h] = shifted
-        field[c, h] = shifted.astype(BF16).reshape(2, 64, 192)
+        for core in range(2):
+            rows = shifted[core].astype(BF16).reshape(64, 192)
+            rows = jnp.dot(order[h], rows, preferred_element_type=F32)
+            field[c, h, core] = rows.astype(BF16)
         field_copy(h).start()
 
     wait_green(0)
     spread_own(0)
+    spread_second(0)
     wait_green(1)
     spread_own(1)
-    turn_given(1)
-    give(1).start()
-    for core in range(2):
-
-        @pl.when(c == core)
-        def _(core=core):
-            turn_full(4, ct.at[2, :, core])
-
-    give(2).start()
-    turn_kept(0)
-    turn_kept(1)
-    load(4).wait()
-    by_walker = dv[...].T.reshape(8, 2, 16, 192)
-    for h in range(2):
-        half_draws = jnp.swapaxes(by_walker[:, h], 0, 1).reshape(8, 2, 8, 192)
-        for core in range(2):
-            dj[h, core] = half_draws[:, core]
     spread_on(0)
     bias_sums(0)
     start_x(0)
+    spread_second(1)
     start_zh(0)
     spread_on(1)
+    start_back(0)
     bias_sums(1)
     start_x(1)
-    start_back(0)
-    start_zh(1)
     shift(0)
     settle(ct.at[:, :, 1 - c], ct_recv)
     field_arrived(0)
@@ -389,20 +437,22 @@
     def half_of(k):
         return k - 8 if k >= 8 else k // 4
 
-    def walk_of(k, i):
-        return 2 * i + half_of(k)
+    def owner_walk(k, i):
+        to_x, to_zh, to_zl = owner(half_of(k), z, i)
+        return to_x * 4 + to_zh, to_zl
 
     def owner_copy(k, i):
         group = group_of(k)
+        walk, zl = owner_walk(k, i)
         return remote(
             turned.at[8 * k + i], operator.at[group, a], o_send, o_recv.at[group],
-            at(walk_of(k, i), y, z, core_of(k)),
+            at(walk, y, zl, core_of(k)),
         )
 
     def each_owner(k, other, own=None):
         def run(d, _):
             i = (a + d) % 8
-            here = jnp.logical_and(walk_of(k, i) == a, core_of(k) == c)
+            here = jnp.logical_and(owner_walk(k, i)[0] == a, core_of(k) == c)
 
             @pl.when(jnp.logical_not(here))
             def _():
@@ -441,26 +491,26 @@
     send_down(0, 0).start()
     send_up(0, 1).start()
     begin(1)
+    start_zh(1)
     multiply_z(0)
     multiply(1, 0, 8)
-    start_back(1)
     pass_on(0)
     begin(2)
+    start_back(1)
     pass_on(1)
     begin(3)
+    over_z(0)
     shift(1)
     field_arrived(1)
     multiply_z(1)
+    pass_on(2)
     multiply(2, 0, 8)
-    over_z(0)
-    pass_on(2)
     begin(4)
+    over_z(1)
     multiply(3, 0, 8)
-    over_z(1)
     pass_on(3)
     begin(5)
     sum_z(8)
-    begin(8)
     by_half = [
         jnp.swapaxes(jnp.swapaxes(dj[h], 0, 1).reshape(16, 8, 192), 0, 1) for h in range(2)
     ]
@@ -472,26 +522,26 @@
     deliver(1)
     over_z(3)
     pass_on(5)
+    begin(7)
     deliver(2)
-    pass_on(8)
-    begin(7)
     deliver(3)
+    sum_z(9)
     over_z(4)
     pass_on(6)
-    sum_z(9)
-    begin(9, 0)
     deliver(4)
     over_z(5)
-    deliver(8)
     pass_on(7)
-    begin(9, 1)
+    begin(8)
+    begin(9)
     deliver(5)
     over_z(6)
+    over_z(7)
+    pass_on(8)
+    deliver(6)
     pass_on(9)
-    over_z(7)
-    deliver(6)
+    deliver(7)
+    deliver(8)
     deliver(9)
-    deliver(7)
 
     settle(gsend.at[pl.ds(0, 15)], a_send)
     settle(ct.at[:, :, c], ct_send)
@@ -531,22 +581,9 @@
     out[0] = total
 
 
-def hand_over(walkers_in, aux_in, walkers_out, aux_out, walkers, aux, sem):
-    ins = [
-        pltpu.make_async_copy(walkers_in, walkers, sem.at[0]),
-        pltpu.make_async_copy(aux_in, aux, sem.at[1]),
-    ]
-    outs = [
-        pltpu.make_async_copy(walkers, walkers_out, sem.at[2]),
-        pltpu.make_async_copy(aux, aux_out, sem.at[3]),
-    ]
-    for copy in ins:
-        copy.start()
-    for copy, following in zip(ins, outs):
-        copy.wait()
-        following.start()
-    for copy in outs:
-        copy.wait()
+def hand_over(walkers_in, aux_in, walkers_out, aux_out):
+    walkers_out[...] = walkers_in[...]
+    aux_out[...] = aux_in[...]
 
 
 def shape(*dims, dtype=BF16):
@@ -579,6 +616,7 @@
             room(40, 192, 128),
             room(3, 8, 2, 192, 640),
             room(2, 8, 192, 640),
+            room(2, 64, 64),
             room(2, 2, 8, 8, 192, dtype=F32),
             room(8, 32, 192),
             room(2, 4, 32, 192),
@@ -605,16 +643,15 @@
             dma(), dma(2), dma(), dma(2), dma(2), dma(10), dma(10), dma(8), dma(), dma(2), dma(), dma(5),
         ],
         compiler_params=pltpu.CompilerParams(
-            collective_id=0, has_side_effects=True, vmem_limit_bytes=60 * 2**20
+            collective_id=0, has_side_effects=True, vmem_limit_bytes=54 * 2**20
         ),
         name="propagate",
     )(walkers, intersection_inverse, aux_draws.T, chol_half, chol_full)
     new_walkers, aux = pl.pallas_call(
         hand_over,
         out_shape=(shape(1, 640, 128, dtype=F32), shape(192, 256, dtype=F32)),
-        in_specs=[ANY] * 2,
-        out_specs=(ANY, ANY),
-        scratch_shapes=[room(1, 640, 128, dtype=F32), room(192, 256, dtype=F32), dma(4)],
+        in_specs=[VMEM] * 2,
+        out_specs=(VMEM, VMEM),
         name="hand_over",
     )(new_walkers, aux)
     return new_walkers, aux.T

time: 112 us -> 104 us (0.929)
  the two profiles are of different devices: /device:TPU:65 before, /device:TPU:8 now
where the time goes in v5:
time: 104 us
  Pallas kernels  104 us (100%)
    pallas_call x1, Pallas kernels, body(): pl.pallas_call(kernel, out_shape=(shape(1, 640, 128, dtype=F32), shape(19...  102 us

profile of v5, /device:TPU:8, one launch (start us, length us, event | category | flops | bytes accessed | tf_op | source)
XLA Modules:
  0.0 104.2 jit_solution(6647019425167640660)
XLA Ops:
  0.6 101.8 %propagate.1 = (f32[1,640,128]{2,1,0:T(8,128)}, f32[192,256]{1,0:T(8,128)}) custom-call(f32[1,640,128]{2,1,0:T(8,128)} %walkers.1, f32[1,128,128]{2,1,0:T(8,128)} %inverse.1, f32[192,256]{1,0:T(8,128)} %bitcast.2, bf16[192,40,128]{2,1,0:T(8,128)(2,1)} %half.1, bf16[192,40,640]{2,1,0:T(8,128)(2,1)} %full.1), custom_call_target="tpu_custom_call" | custom-call | tf_op jit(solution)/shard_map/propagate/pallas_call | solution.py:602
  102.4 1.8 %hand_over.1 = (f32[1,640,128]{2,1,0:T(8,128)}, f32[192,256]{1,0:T(8,128)}) custom-call(f32[1,640,128]{2,1,0:T(8,128)} %get-tuple-element.6.walkers_in, f32[192,256]{1,0:T(8,128)} %get-tuple-element.7.aux_in), custom_call_target="tpu_custom_call" | custom-call | tf_op jit(solution)/shard_map/hand_over/pallas_call | solution.py:650

commit v6 on v5

--- a/solution.py
+++ b/solution.py
@@ -40,7 +40,7 @@
 def kernel(
     walkers, inverse, draws, half, full,
     out, aux_out,
-    wv, iv, dv, hv, fv, gsend, blocks, gt, ht, ct, given, order, dj, pb, xin, zhin, ball, field,
+    wv, iv, dv, hv, fv, gsend, blocks, gt, ht, htk, ct, given, order, dj, pb, xin, zhin, ball, field,
     part, pass_up, pass_down, from_down, from_up, z_out, from_z,
     zin, zsum, z_pass_up, z_pass_down, z_from_down, z_from_up, turned, operator, term1,
     in_sem, ct_send, ct_recv, a_send, a_recv, g_send, g_recv, p_send, p_recv, q_send, q_recv,
@@ -246,10 +246,8 @@
         def step(i, acc):
             p0 = i * 8
             left = jnp.concatenate([gt[h, p0 + q].reshape(128, 128) for q in range(8)], axis=1)
-            right = jnp.concatenate([ht[p0 + q] for q in range(8)], axis=1)
-            return acc + lax.dot_general(
-                left, right, (((1,), (1,)), ((), ())), preferred_element_type=F32
-            )
+            right = htk[pl.ds(p0, 8)].reshape(1024, 192)
+            return acc + jnp.dot(left, right, preferred_element_type=F32)
 
         partial = lax.fori_loop(0, 5, step, jnp.zeros((128, 192), F32))
         pb[4 * h : 4 * h + 4] = partial.astype(BF16).reshape(4, 32, 192)
@@ -305,11 +303,18 @@
             field[c, h, core] = rows.astype(BF16)
         field_copy(h).start()
 
+    def turn_columns(i, _):
+        for q in range(4):
+            htk[4 * i + q] = ht[4 * i + q].astype(F32).T.astype(BF16)
+        return 0
+
     wait_green(0)
     spread_own(0)
+    lax.fori_loop(0, 5, turn_columns, 0)
     spread_second(0)
     wait_green(1)
     spread_own(1)
+    lax.fori_loop(5, 10, turn_columns, 0)
     spread_on(0)
     bias_sums(0)
     start_x(0)
@@ -320,12 +325,10 @@
     bias_sums(1)
     start_x(1)
     shift(0)
-    settle(ct.at[:, :, 1 - c], ct_recv)
-    field_arrived(0)
 
     low, high = pl.ds(0, 4), pl.ds(4, 4)
 
-    def multiply(pair, first_row, last_row):
+    def multiply(pair, first_row=0, last_row=8):
         left = [field[s, pair // 2].reshape(128, 192) for s in range(2)]
 
         def row(r, _):
@@ -347,12 +350,16 @@
             part[8 + h, :, :, r] = value.astype(BF16).reshape(4, 2, 8, 640)
             return 0
 
-        lax.fori_loop(0, 8, row, 0)
-        z_copy(8 + h).start()
+        for rows in (low, high):
+            lax.fori_loop(rows.start, rows.start + 4, row, 0)
+            z_first(8 + h, rows).start()
+
+    def z_first(k, rows):
+        return remote(
+            part.at[k, :, 1 - z, rows], zin.at[k - 8, :, rows], z_send, z_in.at[k - 8], to_z
+        )
 
     def z_copy(k):
-        if k >= 8:
-            return remote(part.at[k, :, 1 - z], zin.at[k - 8], z_send, z_in.at[k - 8], to_z)
         return remote(z_out.at[k], from_z.at[k], z_send, last_in.at[k], to_z)
 
     def sum_z(k):
@@ -451,7 +458,9 @@
 
     def each_owner(k, other, own=None):
         def run(d, _):
-            i = (a + d) % 8
+            turn = d // 2
+            away = jnp.where(turn < 2, 2 + turn, 3 - turn)
+            i = ((x + away) % 4) * 2 + 1 - d % 2
             here = jnp.logical_and(owner_walk(k, i)[0] == a, core_of(k) == c)
 
             @pl.when(jnp.logical_not(here))
@@ -484,6 +493,8 @@
 
         each_owner(k, lambda i: owner_copy(k, i).start(), keep)
 
+    settle(ct.at[:, :, 1 - c], ct_recv)
+    field_arrived(0)
     multiply(0, 0, 4)
     send_up(0, 0).start()
     send_down(0, 1).start()
@@ -493,21 +504,21 @@
     begin(1)
     start_zh(1)
     multiply_z(0)
-    multiply(1, 0, 8)
+    multiply(1)
     pass_on(0)
     begin(2)
     start_back(1)
     pass_on(1)
     begin(3)
+    shift(1)
     over_z(0)
-    shift(1)
     field_arrived(1)
     multiply_z(1)
     pass_on(2)
-    multiply(2, 0, 8)
+    multiply(2)
     begin(4)
     over_z(1)
-    multiply(3, 0, 8)
+    multiply(3)
     pass_on(3)
     begin(5)
     sum_z(8)
@@ -614,6 +625,7 @@
             room(16, 2, 8, 40, 128),
             room(2, 40, 8, 16, 128),
             room(40, 192, 128),
+            room(40, 128, 192),
             room(3, 8, 2, 192, 640),
             room(2, 8, 192, 640),
             room(2, 64, 64),
@@ -643,7 +655,7 @@
             dma(), dma(2), dma(), dma(2), dma(2), dma(10), dma(10), dma(8), dma(), dma(2), dma(), dma(5),
         ],
         compiler_params=pltpu.CompilerParams(
-            collective_id=0, has_side_effects=True, vmem_limit_bytes=54 * 2**20
+            collective_id=0, has_side_effects=True, vmem_limit_bytes=56 * 2**20
         ),
         name="propagate",
     )(walkers, intersection_inverse, aux_draws.T, chol_half, chol_full)

time: 104 us -> 104 us (level)
  no operation moved by 1% of the time
where the time goes in v6:
time: 104 us
  Pallas kernels  103 us (99%)
    pallas_call x1, Pallas kernels, body(): pl.pallas_call(kernel, out_shape=(shape(1, 640, 128, dtype=F32), shape(19...  101 us

profile of v6, /device:TPU:8, one launch (start us, length us, event | category | flops | bytes accessed | tf_op | source)
XLA Modules:
  0.0 103.7 jit_solution(17352191465938832018)
XLA Ops:
  0.6 101.2 %propagate.1 = (f32[1,640,128]{2,1,0:T(8,128)}, f32[192,256]{1,0:T(8,128)}) custom-call(f32[1,640,128]{2,1,0:T(8,128)} %walkers.1, f32[1,128,128]{2,1,0:T(8,128)} %inverse.1, f32[192,256]{1,0:T(8,128)} %bitcast.2, bf16[192,40,128]{2,1,0:T(8,128)(2,1)} %half.1, bf16[192,40,640]{2,1,0:T(8,128)(2,1)} %full.1), custom_call_target="tpu_custom_call" | custom-call | tf_op jit(solution)/shard_map/propagate/pallas_call | solution.py:613
  101.9 1.8 %hand_over.1 = (f32[1,640,128]{2,1,0:T(8,128)}, f32[192,256]{1,0:T(8,128)}) custom-call(f32[1,640,128]{2,1,0:T(8,128)} %get-tuple-element.6.walkers_in, f32[192,256]{1,0:T(8,128)} %get-tuple-element.7.aux_in), custom_call_target="tpu_custom_call" | custom-call | tf_op jit(solution)/shard_map/hand_over/pallas_call | solution.py:662

commit v7 on v6

--- a/solution.py
+++ b/solution.py
@@ -56,9 +56,6 @@
         pair = ((walkers, wv), (inverse, iv), (half, hv), (full, fv), (draws, dv))[index]
         return pltpu.make_async_copy(pair[0], pair[1], in_sem.at[index])
 
-    for index in range(5):
-        load(index).start()
-
     def greet_walk(d, _):
         greet(at((a + d) % 16, y, z, c))
         return 0
@@ -81,6 +78,9 @@
     to_far = at(a, far, z, c)
     for target in (to_far, to_up, to_down, to_z, sibling):
         greet(target)
+
+    for index in range(5):
+        load(index).start()
 
     load(0).wait()
     load(1).wait()
@@ -97,8 +97,12 @@
 
         lax.fori_loop(1, 16, run, 0)
 
+    def away(n):
+        return jnp.where(n < 2, 2 + n, 3 - n)
+
     def peer(d):
-        return (a + d) % 16
+        n = d - 1
+        return ((x + away(n % 4)) % 4) * 4 + (zh + away(n // 4)) % 4
 
     def slot(yy, zz):
         return c * 8 + yy * 2 + zz
@@ -458,9 +462,7 @@
 
     def each_owner(k, other, own=None):
         def run(d, _):
-            turn = d // 2
-            away = jnp.where(turn < 2, 2 + turn, 3 - turn)
-            i = ((x + away) % 4) * 2 + 1 - d % 2
+            i = ((x + away(d % 4)) % 4) * 2 + 1 - d // 4
             here = jnp.logical_and(owner_walk(k, i)[0] == a, core_of(k) == c)
 
             @pl.when(jnp.logical_not(here))

time: 104 us -> 103 us (level)
  no operation moved by 1% of the time
where the time goes in v7:
time: 103 us
  Pallas kernels  102 us (99%)
    pallas_call x1, Pallas kernels, body(): pl.pallas_call(kernel, out_shape=(shape(1, 640, 128, dtype=F32), shape(19...  100 us

profile of v7, /device:TPU:8, one launch (start us, length us, event | category | flops | bytes accessed | tf_op | source)
XLA Modules:
  0.0 102.8 jit_solution(14638492318494226373)
XLA Ops:
  0.6 100.4 %propagate.1 = (f32[1,640,128]{2,1,0:T(8,128)}, f32[192,256]{1,0:T(8,128)}) custom-call(f32[1,640,128]{2,1,0:T(8,128)} %walkers.1, f32[1,128,128]{2,1,0:T(8,128)} %inverse.1, f32[192,256]{1,0:T(8,128)} %bitcast.2, bf16[192,40,128]{2,1,0:T(8,128)(2,1)} %half.1, bf16[192,40,640]{2,1,0:T(8,128)(2,1)} %full.1), custom_call_target="tpu_custom_call" | custom-call | tf_op jit(solution)/shard_map/propagate/pallas_call | solution.py:615
  101.0 1.8 %hand_over.1 = (f32[1,640,128]{2,1,0:T(8,128)}, f32[192,256]{1,0:T(8,128)}) custom-call(f32[1,640,128]{2,1,0:T(8,128)} %get-tuple-element.6.walkers_in, f32[192,256]{1,0:T(8,128)} %get-tuple-element.7.aux_in), custom_call_target="tpu_custom_call" | custom-call | tf_op jit(solution)/shard_map/hand_over/pallas_call | solution.py:664

commit v8 on v7

--- a/solution.py
+++ b/solution.py
@@ -587,11 +587,16 @@
     settle(turned.at[pl.ds(0, 77)], o_send)
     matrix = jnp.swapaxes(operator[...], 0, 1).reshape(640, 640)
     term = term1[...].reshape(640, 128)
-    total = wv[0] + term
+    out[0] = wv[0] + term
+    low_term = term.astype(BF16)
     for degree in range(2, 5):
-        term = jnp.dot(matrix, term.astype(BF16), preferred_element_type=F32) * (1.0 / degree)
-        total = total + term
-    out[0] = total
+        pieces = []
+        for first_row in range(0, 640, 128):
+            rows = matrix[first_row : first_row + 128]
+            value = jnp.dot(rows, low_term, preferred_element_type=F32) * (1.0 / degree)
+            out[0, first_row : first_row + 128] += value
+            pieces.append(value.astype(BF16))
+        low_term = jnp.concatenate(pieces, axis=0)
 
 
 def hand_over(walkers_in, aux_in, walkers_out, aux_out):

time: 103 us -> 103 us (level)
  no operation moved by 1% of the time
where the time goes in v8:
time: 103 us
  Pallas kernels  102 us (99%)
    pallas_call x1, Pallas kernels, body(): pl.pallas_call(kernel, out_shape=(shape(1, 640, 128, dtype=F32), shape(19...  100 us

profile of v8, /device:TPU:8, one launch (start us, length us, event | category | flops | bytes accessed | tf_op | source)
XLA Modules:
  0.0 102.7 jit_solution(2441066299288675533)
XLA Ops:
  0.6 100.2 %propagate.1 = (f32[1,640,128]{2,1,0:T(8,128)}, f32[192,256]{1,0:T(8,128)}) custom-call(f32[1,640,128]{2,1,0:T(8,128)} %walkers.1, f32[1,128,128]{2,1,0:T(8,128)} %inverse.1, f32[192,256]{1,0:T(8,128)} %bitcast.2, bf16[192,40,128]{2,1,0:T(8,128)(2,1)} %half.1, bf16[192,40,640]{2,1,0:T(8,128)(2,1)} %full.1), custom_call_target="tpu_custom_call" | custom-call | tf_op jit(solution)/shard_map/propagate/pallas_call | solution.py:620
  100.9 1.8 %hand_over.1 = (f32[1,640,128]{2,1,0:T(8,128)}, f32[192,256]{1,0:T(8,128)}) custom-call(f32[1,640,128]{2,1,0:T(8,128)} %get-tuple-element.6.walkers_in, f32[192,256]{1,0:T(8,128)} %get-tuple-element.7.aux_in), custom_call_target="tpu_custom_call" | custom-call | tf_op jit(solution)/shard_map/hand_over/pallas_call | solution.py:669
